TPU v7x, 256 devices: a whole 4x4x8 slice. The times are simulated.
256 devices in a mesh: ctx: 32 (over x_lo, z, core), chan: 8 (over x_hi, y).
Axes of the slice: x: 4 (x_hi: 2, x_lo: 2; x = x_hi * 2 + x_lo), y: 4, z: 8, core: 2. Of those that a mesh axis runs over, the one named last changes fastest.
Arguments:
- x_in: bfloat16 [32768, 2048], P('ctx', 'chan'), may hold values from -6 to 6
- conv_weight: float32 [4, 2048], replicated, may hold values from -3 to 3
- proj_weight: bfloat16 [2048, 320], replicated, may hold values from -0.125 to 0.125
- dt_bias: float32 [64], replicated, may hold values from -3 to 0
- decay_log: float32 [64], replicated, may hold values from -20 to -2, as said below
- skip_gain: float32 [64], replicated, may hold values from 0.5 to 1.5
- norm_gain: float32 [2048], P('chan'), may hold values from 0.5 to 1.5
- out_weight: bfloat16 [2048, 2048], P('chan'), may hold values from -0.125 to 0.125
Outputs:
- mixed: bfloat16 [32768, 2048], P('ctx', 'chan')
Inputs may be any that keep to these rules, and one draw needn't show every extreme that they name: A head's decay rate is exp(decay_log).
All inputs are finite; a program needn't handle non-finite values.
Results may differ from a plain program's by a relative error of at most 0.0076.
The roundings to bfloat16 on the way count: a program that leaves them out, or rounds other values in their place, can miss the bound.
Values may be sent and summed in bfloat16 or wider, within the bound.
A program may use at most 128 MiB of HBM per device.

v0:
```python
import jax
import jax.numpy as jnp
from jax import lax
from jax.sharding import PartitionSpec as P


def passed_along(value, axis, steps):
    count = lax.axis_size(axis)
    leading, last = (max(0, -steps), min(count, count - steps))
    return lax.ppermute(value, axis, [(source, source + steps) for source in range(leading, last)])


def carried_in(part, axis, combine, identity):
    place = lax.axis_index(axis)
    gathered = jax.tree.map(lambda a: lax.all_gather(a, axis), part)
    state = jax.tree.map(lambda a, e: jnp.zeros_like(a) + jnp.asarray(e, a.dtype), part, identity)

    def one(hop, state):
        return combine(
            state, jax.tree.map(lambda a: lax.dynamic_index_in_dim(a, hop, 0, False), gathered)
        )

    return lax.fori_loop(0, place, one, state)


def link_states(earlier, latter):
    return (earlier[0] * latter[0], latter[0][..., None, None] * earlier[1] + latter[1])


def reverse_slots(block_data, row_parts, col_parts):
    rows, cols = block_data.shape
    split = block_data.reshape(row_parts, rows // row_parts, col_parts, cols // col_parts)
    return jnp.flip(split, (0, 2)).reshape(rows, cols)


def mirrored_input(block_data):
    row_parts = lax.axis_size("ctx")
    col_parts = lax.axis_size("chan")
    moved = lax.all_to_all(
        lax.all_to_all(
            jnp.flip(block_data, (0, 1)), "ctx", split_axis=0, concat_axis=0, tiled=True
        ),
        "chan",
        split_axis=1,
        concat_axis=1,
        tiled=True,
    )
    moved = reverse_slots(moved, row_parts, col_parts)
    return lax.all_to_all(
        lax.all_to_all(moved, "ctx", split_axis=0, concat_axis=0, tiled=True),
        "chan",
        split_axis=1,
        concat_axis=1,
        tiled=True,
    )


def mirrored_output(block_data):
    row_parts = lax.axis_size("ctx")
    col_parts = lax.axis_size("chan")
    moved = lax.all_to_all(
        lax.all_to_all(
            jnp.flip(block_data, (0, 1)), "ctx", split_axis=0, concat_axis=0, tiled=True
        ),
        "chan",
        split_axis=1,
        concat_axis=1,
        tiled=True,
    )
    moved = reverse_slots(moved, row_parts, col_parts)
    return lax.all_to_all(
        lax.all_to_all(moved, "ctx", split_axis=0, concat_axis=0, tiled=True),
        "chan",
        split_axis=1,
        concat_axis=1,
        tiled=True,
    )


def block_pass(conv_out, b_rows, c_rows, rates, decay):
    row_count, local_width = conv_out.shape
    heads = rates.shape[1]
    head_dim = local_width // heads
    block_len = min(256, row_count)
    block_count = row_count // block_len
    x_blocks = conv_out.reshape(block_count, block_len, heads, head_dim)
    b_blocks = b_rows.reshape(block_count, block_len, -1)
    c_blocks = c_rows.reshape(block_count, block_len, -1)
    a_blocks = (rates * decay[None, :]).reshape(block_count, block_len, heads)
    dt_blocks = rates.reshape(block_count, block_len, heads)
    lower = jnp.arange(block_len)[:, None] >= jnp.arange(block_len)[None, :]

    def advance(carry, item):
        carried, offset = carry
        x_block, b_block, c_block, a_block, dt_block = item
        x_wide = x_block.astype(jnp.float32)
        cumul = jnp.cumsum(a_block, axis=0)
        scores = lax.dot_general(
            c_block, b_block, (((1,), (1,)), ((), ())), preferred_element_type=jnp.float32
        )
        segment = cumul[:, None, :] - cumul[None, :, :]
        weights = jnp.exp(jnp.where(lower[:, :, None], segment, -jnp.inf))
        weights = scores[:, :, None] * weights * dt_block[None, :, :]
        inner = jnp.einsum("tsh,shp->thp", weights, x_wide, precision=lax.Precision.HIGHEST)
        c_wide = c_block.astype(jnp.float32)
        outer = jnp.exp(cumul)[:, :, None] * jnp.einsum(
            "tn,hnp->thp", c_wide, carried, precision=lax.Precision.HIGHEST
        )
        tail = jnp.exp(cumul[-1][None, :] - cumul) * dt_block
        b_wide = b_block.astype(jnp.float32)
        fresh = jnp.einsum(
            "sn,shp->hnp", b_wide, x_wide * tail[:, :, None], precision=lax.Precision.HIGHEST
        )
        updated = jnp.exp(cumul[-1])[:, None, None] * carried + fresh
        return ((updated, offset + cumul[-1]), (inner + outer, offset[None, :] + cumul))

    start_state = jnp.zeros((heads, b_rows.shape[1], head_dim), jnp.float32)
    start_offset = jnp.zeros((heads,), jnp.float32)
    (final_state, final_offset), (outputs, cumdev) = lax.scan(
        advance, (start_state, start_offset), (x_blocks, b_blocks, c_blocks, a_blocks, dt_blocks)
    )
    summary = (jnp.exp(final_offset), final_state)
    return (outputs.reshape(row_count, heads, head_dim), cumdev.reshape(row_count, heads), summary)


def finish(local_out, cumdev, c_rows, entering, conv_out, skip):
    carried = jnp.einsum(
        "tn,hnp->thp", c_rows.astype(jnp.float32), entering, precision=lax.Precision.HIGHEST
    )
    result = local_out + jnp.exp(cumdev)[:, :, None] * carried
    row_count, heads, head_dim = result.shape
    result = result + skip[None, :, None] * conv_out.reshape(row_count, heads, head_dim).astype(
        jnp.float32
    )
    return result.reshape(row_count, heads * head_dim)


def shards(x_in, conv_weight, proj_weight, dt_bias, decay_log, skip_gain, norm_gain, out_weight):
    row_count, local_width = x_in.shape
    total_width = conv_weight.shape[1]
    reach = conv_weight.shape[0] - 1
    heads_all = dt_bias.shape[0]
    state_size = (proj_weight.shape[1] - heads_all) // 2
    heads_local = heads_all * local_width // total_width
    chan_pos = lax.axis_index("chan")
    chan_first = chan_pos * local_width
    head_first = chan_pos * heads_local
    own_conv = lax.dynamic_slice_in_dim(conv_weight, chan_first, local_width, 1)
    own_proj = lax.dynamic_slice_in_dim(proj_weight, chan_first, local_width, 0)
    own_decay = -jnp.exp(lax.dynamic_slice_in_dim(decay_log, head_first, heads_local, 0))
    own_skip = lax.dynamic_slice_in_dim(skip_gain, head_first, heads_local, 0)

    def heads_of(proj, offsets):
        rates = jax.nn.softplus(proj[:, 2 * state_size :] + offsets[None, :])
        b_rows = proj[:, :state_size].astype(jnp.bfloat16)
        c_rows = proj[:, state_size : 2 * state_size].astype(jnp.bfloat16)
        return (b_rows, c_rows, lax.dynamic_slice_in_dim(rates, head_first, heads_local, 1))

    def conv_silu(padded_rows, taps):
        summed = jnp.zeros((row_count, local_width), jnp.float32)
        for tap_index in range(reach + 1):
            summed = summed + taps[tap_index][None, :] * padded_rows[
                tap_index : tap_index + row_count
            ].astype(jnp.float32)
        return jax.nn.silu(summed).astype(jnp.bfloat16)

    x_mirror = mirrored_input(x_in)
    stacked = jnp.stack((x_in, x_mirror))
    incoming = passed_along(stacked[:, row_count - reach :], "ctx", 1)
    padded = jnp.concatenate([incoming, stacked], 1)
    fwd_x = conv_silu(padded[0], own_conv)
    rev_x = conv_silu(padded[1], own_conv)
    fwd_proj = jnp.dot(fwd_x, own_proj, preferred_element_type=jnp.float32)
    rev_proj = jnp.dot(rev_x, own_proj, preferred_element_type=jnp.float32)
    fwd_proj, rev_proj = lax.psum((fwd_proj, rev_proj), "chan")
    fwd_b, fwd_c, fwd_dt = heads_of(fwd_proj, dt_bias)
    rev_b, rev_c, rev_dt = heads_of(rev_proj, dt_bias)
    fwd_local, fwd_cum, fwd_summary = block_pass(fwd_x, fwd_b, fwd_c, fwd_dt, own_decay)
    rev_local, rev_cum, rev_summary = block_pass(rev_x, rev_b, rev_c, rev_dt, own_decay)
    paired = (
        jnp.stack((fwd_summary[0], rev_summary[0])),
        jnp.stack((fwd_summary[1], rev_summary[1])),
    )
    neutral = (jnp.ones_like(paired[0]), jnp.zeros_like(paired[1]))
    entering = carried_in(paired, "ctx", link_states, neutral)
    forward_out = finish(fwd_local, fwd_cum, fwd_c, entering[1][0], fwd_x, own_skip)
    mirror_out = finish(rev_local, rev_cum, rev_c, entering[1][1], rev_x, own_skip)
    reverse_out = mirrored_output(mirror_out)
    combined = forward_out + reverse_out
    squares = jnp.sum(combined * combined, axis=1)
    totals = lax.psum(squares, "chan")
    scaling = lax.rsqrt(totals / total_width + 1e-05)
    normed = (combined * scaling[:, None] * norm_gain[None, :]).astype(jnp.bfloat16)
    result = lax.psum_scatter(
        lax.dot_general(
            out_weight, normed, (((0,), (1,)), ((), ())), preferred_element_type=jnp.float32
        ),
        "chan",
        scatter_dimension=0,
        tiled=True,
    ).T
    return result.astype(jnp.bfloat16)


def solution(mesh):
    in_specs = (P("ctx", "chan"), P(), P(), P(), P(), P(), P("chan"), P("chan", None))
    out_specs = P("ctx", "chan")
    return jax.shard_map(shards, mesh=mesh, in_specs=in_specs, out_specs=out_specs, check_vma=False)
```

profile of v0, /device:TPU:1, one launch (start us, length us, event | category | flops | bytes accessed | tf_op | source)
XLA Modules:
  0.0 739.0 jit_solution(7738414816796200922)
XLA Ops:
  6.5 7.1 rev.16
  13.6 27.5 %all_to_all.72 = bf16[32,32,256]{2,1,0:T(8,128)(2,1)} all-to-all(bf16[32,32,256]{2,1,0:T(8,128)(2,1)S(1)} %bitcast.329), channel_id=1, replica_groups=mesh['ctx'=32,'chan'=8] {'ctx'}, dimensions={0} | all-to-all | bytes 1048576 | tf_op jit(solution)/shard_map/all_to_all | solution.py:40
  41.2 2.6 all_to_all.50
  43.8 2.1 copy.107
  46.0 15.6 %all_to_all.73 = bf16[1024,8,32]{0,2,1:T(8,128)(2,1)} all-to-all(bf16[1024,8,32]{0,2,1:T(8,128)(2,1)} %copy.107), channel_id=1, replica_groups=mesh['ctx'=32,'chan'=8] {'chan'}, dimensions={1} | all-to-all | bytes 1048576 | tf_op jit(solution)/shard_map/all_to_all | solution.py:39
  61.5 2.8 reshape.293
  64.4 3.2 rev.17
  67.6 2.8 copy.145
  70.4 23.5 %all_to_all.74 = bf16[32,32,256]{2,1,0:T(8,128)(2,1)} all-to-all(bf16[32,32,256]{2,1,0:T(8,128)(2,1)S(1)} %copy.145), channel_id=1, replica_groups=mesh['ctx'=32,'chan'=8] {'ctx'}, dimensions={0} | all-to-all | bytes 1048576 | tf_op jit(solution)/shard_map/all_to_all | solution.py:50
  93.9 2.6 all_to_all.54
  96.5 2.1 copy.109
  98.7 3.6 all-to-all-start.3
  102.3 8.7 %all-to-all-done.3 = bf16[1024,8,32]{0,2,1:T(8,128)(2,1)S(1)} async-done(((bf16[1024,8,32]{0,2,1:T(8,128)(2,1)}), bf16[1024,8,32]{0,2,1:T(8,128)(2,1)S(1)}, u32[]{:S(2)}, u32[]{:S(2)}) %all-to-all-start.3) | async-done | bytes 524320 | tf_op jit(solution)/shard_map/all_to_all | solution.py:49
  111.3 6.7 collective-permute-start
  121.2 2.5 copy.119
  125.1 1.9 fusion.102
  127.0 1.9 fusion.103
  132.8 2.8 slice_convert_fusion.5
  144.7 1.6 copy.120
  153.9 5.4 fusion.100
  161.0 58.6 %all-reduce.3.cloned.1.call-done = (f32[1024,320]{0,1:T(8,128)}, f32[1024,320]{0,1:T(8,128)}) async-done(((f32[1024,320]{0,1:T(8,128)}, f32[1024,320]{0,1:T(8,128)}), (f32[1024,320]{0,1:T(8,128)}, f32[1024,320]{0,1:T(8,128)})) %all-reduce.3.cloned.1.call-update) | async-done | bytes 2621456 | tf_op jit(solution)/shard_map/psum | solution.py:175
  224.0 42.1 %while.47 = (s32[]{:T(128)}, f32[8,128,32]{1,2,0:T(8,128)S(1)}, f32[8]{0:T(128)}, f32[4,256,8,32]{1,0,3,2:T(4,128)S(1)}, f32[4,256,8]{1,2,0:T(8,128)S(1)}, /*ind...) while((s32[]{:T(128)}, f32[8,128,32]{1,2,0:T(8,128)S(1)}, ...), condition=%wide.region_4.5_spmd.clone, body=%wide.region_1.4_spmd.clone.sunk | while | flops 422221888 | bytes 3814757 | solution.py:119
  225.7 2.5 fusion.168
  228.5 3.4 dynamic_update_slice.25
  235.9 2.5 fusion.168
  238.8 3.4 dynamic_update_slice.25
  246.7 2.5 fusion.168
  249.6 3.4 dynamic_update_slice.25
  257.6 2.5 fusion.168
  260.4 3.4 dynamic_update_slice.25
  269.1 49.2 %while.48 = (s32[]{:T(128)}, f32[8,128,32]{1,2,0:T(8,128)S(1)}, f32[8]{0:T(128)S(1)}, f32[4,256,8,32]{1,0,3,2:T(4,128)}, f32[4,256,8]{1,2,0:T(8,128)S(1)}, /*ind...) while((s32[]{:T(128)}, f32[8,128,32]{1,2,0:T(8,128)S(1)}, ...), condition=%wide.region_9.10_spmd.clone, body=%wide.region_6.9_spmd.clone.sunk | while | flops 422221888 | bytes 3814757 | solution.py:119
  270.8 2.5 fusion.181
  273.7 6.5 dynamic_update_slice.27
  283.1 2.5 fusion.181
  286.0 6.5 dynamic_update_slice.27
  295.4 2.5 fusion.181
  298.3 6.5 dynamic_update_slice.27
  307.7 2.5 fusion.181
  310.6 6.5 dynamic_update_slice.27
  319.2 2.8 reshape.303
  322.5 39.2 %all-gather.2 = f32[32,2,8]{2,1,0:T(2,128)S(1)} all-gather(f32[1,2,8]{2,1,0:T(2,128)S(1)} %maximum_bitcast_fusion), channel_id=2, replica_groups=mesh['ctx'=32,'chan'=8] {'ctx'}, dimensions={0}, use_global_device_ids=true | all-gather | bytes 2112 | tf_op jit(solution)/shard_map/all_gather | solution.py:15
  361.8 33.6 %all-gather.5.cloned.1.call-done = f32[64,8,128,32]{2,3,1,0:T(8,128)} async-done(((f32[2,8,128,32]{2,3,1,0:T(8,128)}), f32[64,8,128,32]{2,3,1,0:T(8,128)}) %all-gather.5.cloned.1.call-update) | async-done | bytes 8388624 | tf_op jit(solution)/shard_map/all_gather | solution.py:15
  395.5 1.6 while.46
  397.4 1.6 fusion.111
  399.1 3.3 multiply_add_fusion
  405.3 77.4 %all_to_all.75 = f32[32,32,256]{2,1,0:T(8,128)S(1)} all-to-all(f32[32,32,256]{2,1,0:T(8,128)S(1)} %bitcast.321), channel_id=1, replica_groups=mesh['ctx'=32,'chan'=8] {'ctx'}, dimensions={0} | all-to-all | bytes 2097152 | tf_op jit(solution)/shard_map/all_to_all | solution.py:62
  482.7 2.4 all_to_all.58
  485.1 2.8 copy.140
  487.9 20.2 %all_to_all.76 = f32[1024,8,32]{0,2,1:T(8,128)S(1)} all-to-all(f32[1024,8,32]{0,2,1:T(8,128)S(1)} %copy.140), channel_id=1, replica_groups=mesh['ctx'=32,'chan'=8] {'chan'}, dimensions={1} | all-to-all | bytes 2097152 | tf_op jit(solution)/shard_map/all_to_all | solution.py:61
  508.2 2.7 reshape.305
  510.9 6.6 rev.19
  517.5 3.5 copy.150
  521.0 35.5 %all_to_all.77 = f32[32,32,256]{2,1,0:T(8,128)S(1)} all-to-all(f32[32,32,256]{2,1,0:T(8,128)S(1)} %copy.150), channel_id=1, replica_groups=mesh['ctx'=32,'chan'=8] {'ctx'}, dimensions={0} | all-to-all | bytes 2097152 | tf_op jit(solution)/shard_map/all_to_all | solution.py:72
  556.5 2.4 all_to_all.62
  558.9 3.7 copy.142
  562.6 4.4 all-to-all-start.7
  567.1 2.9 reshape.298
  570.0 2.5 fusion.113
  572.5 7.5 %all-to-all-done.7 = f32[1024,8,32]{0,2,1:T(8,128)} async-done(((f32[1024,8,32]{0,2,1:T(8,128)}), f32[1024,8,32]{0,2,1:T(8,128)}, u32[]{:S(2)}, u32[]{:S(2)}) %all-to-all-start.7) | async-done | bytes 1048608 | tf_op jit(solution)/shard_map/all_to_all | solution.py:71
  580.0 3.9 multiply_reduce_fusion
  583.9 21.4 %psum.23 = f32[1024]{0:T(1024)S(1)} all-reduce(f32[1024]{0:T(1024)S(1)} %get-tuple-element.408), channel_id=1, replica_groups=mesh['ctx'=32,'chan'=8] {'chan'}, use_global_device_ids=true, to_apply=%region_13.14 | all-reduce | flops 1024 | bytes 8192 | tf_op jit(solution)/shard_map/psum | solution.py:191
  606.7 4.5 convolution_bitcast_fusion.2
  611.2 119.2 %reduce-scatter.2.cloned.1.call-done = f32[256,1024]{0,1:T(8,128)} async-done(((f32[2048,1024]{0,1:T(8,128)}), f32[256,1024]{0,1:T(8,128)}) %reduce-scatter.2.cloned.1.call-update) | async-done | bytes 1048592 | tf_op jit(solution)/shard_map/reduce_scatter | solution.py:194
  730.4 2.1 convert_bitcast_fusion
  (265 shorter events, 72.6 us)
Async XLA Ops:
  6.5 118.5 %copy-start = (bf16[2048,320]{0,1:T(8,128)(2,1)S(1)}, bf16[2048,320]{0,1:T(8,128)(2,1)}, u32[]{:S(2)}) copy-start(bf16[2048,320]{0,1:T(8,128)(2,1)} %param.16) | copy-start | bytes 3932164
  98.7 12.6 %copy-start.14 = (bf16[1024,256]{1,0:T(8,128)(2,1)S(1)}, bf16[1024,256]{1,0:T(8,128)(2,1)}, u32[]{:S(2)}) copy-start(bf16[1024,256]{1,0:T(8,128)(2,1)} %param.14) | copy-start | bytes 1572868
  98.7 12.4 %all-to-all-start.3 = ((bf16[1024,8,32]{0,2,1:T(8,128)(2,1)}), bf16[1024,8,32]{0,2,1:T(8,128)(2,1)S(1)}, u32[]{:S(2)}, u32[]{:S(2)}) async-start(bf16[1024,8,32]{0,2,1:T(8,128)(2,1)} %copy.109), calls=%async_computation.3 | async-start | bytes 1048576 | tf_op jit(solution)/shard_map/all_to_all | solution.py:49
  102.3 117.3 %all-reduce.3.cloned.1.call-start = ((), (), s32[]{:S(2)}) async-start(), calls=%async_computation.11 | async-start | bytes 5242880 | tf_op jit(solution)/shard_map/psum | solution.py:175
  111.3 12.5 %copy-start.15 = (bf16[1,1024,256]{2,1,0:T(8,128)(2,1)}, bf16[1,1024,256]{2,1,0:T(8,128)(2,1)S(1)}, u32[]{:S(2)}) copy-start(bf16[1,1024,256]{2,1,0:T(8,128)(2,1)S(1)} %copy.110) | copy-start | bytes 1572868
  111.3 12.5 %collective-permute-start = (bf16[2,3,256]{2,1,0:T(4,128)(2,1)S(1)}, bf16[2,3,256]{2,1,0:T(4,128)(2,1)S(1)}, u32[]{:S(2)}, u32[]{:S(2)}) collective-permute-start(bf16[2,3,256]{2,1,0:T(4,128)(2,1)S(1)} %pad_maximum_fusion.1), channel_id=1, source_target_pairs={{0,8},{8,16},{16,24},{24,32},{32,40},{40,48},{48,56},{56,64},{64,7... | collective-permute-start | bytes 9224 | tf_op jit(solution)/shard_map/ppermute | solution.py:10
  125.1 2.0 copy-start.20
  129.0 2.3 copy-start.32
  129.0 266.4 %all-gather.5.cloned.1.call-start = ((), (), s32[]{:S(2)}) async-start(), calls=%async_computation.10 | async-start | bytes 8650752 | tf_op jit(solution)/shard_map/all_gather | solution.py:15
  129.4 6.2 copy-start.7
  129.7 24.2 %copy-start.23 = (f32[8,32]{1,0:T(8,128)}, f32[8,32]{1,0:T(8,128)S(1)}, u32[]{:S(2)}) copy-start(f32[8,32]{1,0:T(8,128)S(1)} %mul.355) | copy-start | bytes 3076
  129.8 24.1 %copy-start.25 = (f32[8,32]{1,0:T(8,128)}, f32[8,32]{1,0:T(8,128)S(1)}, u32[]{:S(2)}) copy-start(f32[8,32]{1,0:T(8,128)S(1)} %mul.358) | copy-start | bytes 3076
  137.1 3.1 copy-start.9
  140.2 3.0 copy-start.11
  143.3 1.5 copy-start.13
  146.3 3.0 copy-start.2
  149.3 3.0 copy-start.4
  152.4 6.9 copy-start.6
  161.0 61.2 %copy-start.31 = (f32[64]{0:T(128)S(1)}, f32[64]{0:T(128)}, u32[]{:S(2)}) copy-start(f32[64]{0:T(128)} %param.17) | copy-start | bytes 772
  219.6 1.7 copy-start.18
  221.2 2.4 copy-start.17
  266.1 3.0 copy-start.16
  266.1 3.0 copy-start.21
  266.1 3.0 copy-start.27
  269.1 50.0 %copy-start.33 = (f32[64]{0:T(128)S(1)}, f32[64]{0:T(128)}, u32[]{:S(2)}) copy-start(f32[64]{0:T(128)} %param.19) | copy-start | bytes 772
  319.2 79.9 %copy-start.28 = (f32[8]{0:T(128)}, f32[8]{0:T(128)S(1)}, u32[]{:S(2)}) copy-start(f32[8]{0:T(128)S(1)} %dynamic_slice.66) | copy-start | bytes 100
  397.1 2.0 copy-start.3
  397.1 2.0 copy-start.24
  397.1 2.0 copy-start.26
  397.4 1.7 copy-start.5
  562.6 7.4 copy-start.22
  562.6 17.4 %all-to-all-start.7 = ((f32[1024,8,32]{0,2,1:T(8,128)}), f32[1024,8,32]{0,2,1:T(8,128)}, u32[]{:S(2)}, u32[]{:S(2)}) async-start(f32[1024,8,32]{0,2,1:T(8,128)} %copy.142), calls=%async_computation.7 | async-start | bytes 2097152 | tf_op jit(solution)/shard_map/all_to_all | solution.py:71
  567.0 13.0 %copy-start.8 = (f32[1024,256]{0,1:T(8,128)S(1)}, f32[1024,256]{0,1:T(8,128)}, u32[]{:S(2)}) copy-start(f32[1024,256]{0,1:T(8,128)} %copy-done.7) | copy-start | bytes 3145732
  567.0 13.0 %copy-start.10 = (f32[1,1024,256]{1,2,0:T(8,128)S(1)}, f32[1,1024,256]{1,2,0:T(8,128)}, u32[]{:S(2)}) copy-start(f32[1,1024,256]{1,2,0:T(8,128)} %copy-done.9) | copy-start | bytes 3145732
  567.0 13.0 %copy-start.12 = (f32[1,1024,256]{1,2,0:T(8,128)S(1)}, f32[1,1024,256]{1,2,0:T(8,128)}, u32[]{:S(2)}) copy-start(f32[1,1024,256]{1,2,0:T(8,128)} %copy-done.11) | copy-start | bytes 3145732
  567.0 12.9 %copy-start.29 = (f32[8]{0:T(128)S(1)}, f32[8]{0:T(128)}, u32[]{:S(2)}) copy-start(f32[8]{0:T(128)} %copy-done.28) | copy-start | bytes 100
  567.0 163.4 %reduce-scatter.2.cloned.1.call-start = ((), (), s32[]{:S(2)}) async-start(), calls=%async_computation.9 | async-start | bytes 9437184 | tf_op jit(solution)/shard_map/reduce_scatter | solution.py:194
  580.0 25.3 %copy-start.30 = (f32[256]{0:T(256)S(1)}, f32[256]{0:T(256)}, u32[]{:S(2)}) copy-start(f32[256]{0:T(256)} %param.20) | copy-start | bytes 3076
  583.9 22.8 %copy-start.19 = (bf16[256,2048]{1,0:T(8,128)(2,1)S(1)}, bf16[256,2048]{1,0:T(8,128)(2,1)}, u32[]{:S(2)}) copy-start(bf16[256,2048]{1,0:T(8,128)(2,1)} %param.21) | copy-start | bytes 3145732
  611.2 121.2 %copy-start.1 = (bf16[2048,320]{0,1:T(8,128)(2,1)S(1)}, bf16[2048,320]{0,1:T(8,128)(2,1)}, u32[]{:S(2)}) copy-start(bf16[2048,320]{0,1:T(8,128)(2,1)} %param.16) | copy-start | bytes 3932164
Sparse Core Ops, SparseCore 0:
  129.1 90.5 all-reduce.2
  319.2 76.1 all-gather.4
  611.3 118.9 reduce-scatter.1
where the time goes:
time: 743 us; the launch traced here: 739 us
  blocking collectives  260 us (35%)
  waiting for transfers between devices  228 us (31%)
  local copies, waits for them, and re-layouts  137 us (18%)
  matrix products  46.1 us (6%)
  other arithmetic  38.2 us (5%)
  starting transfers between devices  15.1 us (2%)
  between operations  13.8 us (2%)
    reduce_scatter x1, waiting for transfers between devices, shards(): lax.psum_scatter(lax.dot_general(out_weight, normed, (((0,), (1,)), ((),...  119 us
    all_to_all x1, blocking collectives, mirrored_output(): lax.all_to_all(jnp.flip(block_data, (0, 1)), 'ctx', split_axis=0, concat_...  77.4 us
    psum x1, waiting for transfers between devices, shards(): fwd_proj, rev_proj = lax.psum((fwd_proj, rev_proj), 'chan')  58.6 us
    dynamic_update_slice x16, local copies, waits for them, and re-layouts, block_pass(): lax.scan(advance, (start_state, start_offset), (x_blocks, b_blocks, c_blo...  41.7 us
    all_gather x1, blocking collectives, carried_in(): gathered = jax.tree.map(lambda a: lax.all_gather(a, axis), part)  39.2 us
    all_to_all x1, blocking collectives, mirrored_output(): lax.all_to_all(moved, 'ctx', split_axis=0, concat_axis=0, tiled=True)  35.5 us
    all_gather x1, waiting for transfers between devices, carried_in(): gathered = jax.tree.map(lambda a: lax.all_gather(a, axis), part)  33.6 us
    all_to_all x1, blocking collectives, mirrored_input(): lax.all_to_all(jnp.flip(block_data, (0, 1)), 'ctx', split_axis=0, concat_...  27.5 us
  transfers between devices with their start and end apart: 6, of which 5 were waited for; matrix products, arithmetic and copies ran while one was open for 6% of the time, Pallas kernels for 0%

commit v1 on v0

v1 whole, which is shorter than its diff:
```python
import functools

import jax
import jax.numpy as jnp
from jax import lax
from jax.experimental import pallas as pl
from jax.experimental.pallas import tpu as pltpu
from jax.sharding import PartitionSpec as P

F32 = jnp.float32
BF16 = jnp.bfloat16
MESH = pl.DeviceIdType.MESH
EPS = 1e-05
GROUP = 4


def mm(a, b, dims=((1,), (0,)), **kw):
    return lax.dot_general(a, b, (dims, ((), ())), preferred_element_type=F32, **kw)


def silu(v):
    return v / (1.0 + jnp.exp(-v))


def iota(shape, axis):
    return lax.broadcasted_iota(jnp.int32, shape, axis)


def kernel(
    dims,
    x_ref, cw_ref, pw_ref, prm_ref, gain_ref, w_ref, out_ref,
    xpad, xe, cbuf, cwr, xf, xr, bc, dtout, dtin, cumr, cumc, ldr, fresh, dch, yacc,
    mcat, xbd, emat, sxs, sxr, sys_, syr, stin, comb_s, comb_r, gall, wbuf, acc, obs, obr,
    xa_s, xa_r, ha_s, ha_r, g_s, g_r, w_s, w_r, wf_s, wf_r, bc_s, bc_r, dt_s, dt_r,
    sx_s, sx_r, sy_s, sy_r, cb_s, cb_r, ob_s, ob_r,
):
    NC, NJ, T, CW, D, N, HL, PP = dims
    SR = T // NJ
    HALVES = CW // 128
    RB = T // GROUP
    WC = GROUP * CW
    i = lax.axis_index("ctx")
    j = lax.axis_index("chan")
    prev_i = lax.rem(i + NC - 1, NC)
    next_i = lax.rem(i + 1, NC)
    core = lax.rem(i, 2)
    sib = i + 1 - 2 * core
    xh = j // GROUP
    yy = lax.rem(j, GROUP)

    def at(ci, cj):
        return {"ctx": ci, "chan": cj}

    def to(k):
        return lax.rem(j + k, NJ)

    def frm(k):
        return lax.rem(j + NJ - k, NJ)

    def rcopy(src, dst, ss, rs, dev):
        return pltpu.make_async_remote_copy(
            src_ref=src, dst_ref=dst, send_sem=ss, recv_sem=rs, device_id=dev, device_id_type=MESH
        )

    barrier = pltpu.get_barrier_semaphore()

    def hail(dev):
        pl.semaphore_signal(barrier, inc=1, device_id=dev, device_id_type=MESH)

    for k in range(1, NJ):
        hail(at(i, to(k)))

    def hail_ctx(k, c):
        hail(at(lax.rem(i + k, NC), j))
        return c

    lax.fori_loop(1, NC, hail_ctx, 0)

    @pl.when(j == 0)
    def _():
        for q in range(NJ):
            hail(at(prev_i, q))

    @pl.when(j == NJ - 1)
    def _():
        for q in range(NJ):
            hail(at(next_i, q))

    def win(jd):
        return pl.multiple_of(jnp.clip(SR * jd - 16, 0, T - SR - 32), 16)

    xpad[16:16 + T, :] = x_ref[...]
    xe[j, 16:SR + 48, :] = x_ref[pl.ds(win(j), SR + 32), :]
    gall[j] = gain_ref[...]
    wbuf[j] = w_ref[:, pl.ds(pl.multiple_of(xh * WC, 128), WC)]
    anti = iota((CW, CW), 0) + iota((CW, CW), 1) == CW - 1
    anti_f = jnp.where(anti, 1.0, 0.0).astype(F32)
    anti_b = anti_f.astype(BF16)
    for b in range(NJ):
        cwr[:, b * CW:(b + 1) * CW] = mm(
            cw_ref[:, (NJ - 1 - b) * CW:(NJ - b) * CW], anti_f, precision=lax.Precision.HIGHEST
        )
    er = lax.rem(iota((6 * HL, 2 * CW), 0), 2 * HL)
    ec = iota((6 * HL, 2 * CW), 1)
    head_of = ec // (CW // HL)
    target = jnp.where(head_of < HL, head_of, 3 * HL - 1 - head_of)
    emat[...] = jnp.where(er == target, 1.0, 0.0).astype(BF16)

    def expand(rows):
        hi = rows.astype(BF16)
        rest = rows - hi.astype(F32)
        mid = rest.astype(BF16)
        low = (rest - mid.astype(F32)).astype(BF16)
        return mm(jnp.concatenate([hi, mid, low], axis=0), emat[...], ((0,), (0,)))

    pl.semaphore_wait(barrier, NJ - 1 + NC - 1 + 2)

    def xa(k, jd):
        return rcopy(
            x_ref.at[pl.ds(win(jd), SR + 32), :], xe.at[j, pl.ds(16, SR + 32), :],
            xa_s.at[k], xa_r.at[k], at(i, jd),
        )

    def xa_in(k):
        return rcopy(
            x_ref.at[pl.ds(0, SR + 32), :], xe.at[frm(k), pl.ds(16, SR + 32), :],
            xa_s.at[k], xa_r.at[k], at(i, frm(k)),
        )

    lastrows, firstrows = x_ref.at[pl.ds(T - 16, 16), :], x_ref.at[pl.ds(0, 16), :]
    halo = [
        rcopy(lastrows, xpad.at[pl.ds(0, 16), :], ha_s.at[0], ha_r.at[0], at(next_i, j)),
        rcopy(firstrows, xpad.at[pl.ds(16 + T, 16), :], ha_s.at[1], ha_r.at[1], at(prev_i, j)),
    ]
    slab_pre = rcopy(
        lastrows, xe.at[j, pl.ds(0, 16), :], ha_s.at[2], ha_r.at[2 + j], at(next_i, 0)
    )
    slab_post = rcopy(
        firstrows, xe.at[j, pl.ds(SR + 48, 16), :], ha_s.at[3], ha_r.at[2 + j], at(prev_i, NJ - 1)
    )
    slab_pre.start()
    slab_post.start()
    for k in range(1, NJ):
        xa(k, to(k)).start()
    for h in halo:
        h.start()
    gains = [
        rcopy(gall.at[j], gall.at[j], g_s.at[k], g_r.at[k], at(i, to(k))) for k in range(1, NJ)
    ]
    for g in gains:
        g.start()

    def conv_pair(taps, rtaps):
        vf = taps[0:1, :] * cbuf[13:13 + SR, :]
        vr = rtaps[0:1, :] * cbuf[19:19 + SR, :]
        for k in range(1, 4):
            vf = vf + taps[k:k + 1, :] * cbuf[13 + k:13 + k + SR, :]
            vr = vr + rtaps[k:k + 1, :] * cbuf[19 - k:19 - k + SR, :]
        return silu(vf).astype(BF16), silu(vr).astype(BF16)

    own_cols = pl.ds(pl.multiple_of(j * CW, 128), CW)

    def own_conv(c, carry):
        rows = pl.ds(pl.multiple_of(c * SR, 16), SR)
        cbuf[...] = xpad[pl.ds(pl.multiple_of(c * SR, 16), SR + 32), :].astype(F32)
        f, r = conv_pair(cw_ref[:, own_cols], cwr[:, own_cols])
        xf[rows, :] = f
        xr[rows, :] = r
        return carry

    lax.fori_loop(1, NJ - 1, own_conv, 0)

    @pl.when(j == 0)
    def _():
        for q in range(NJ):
            rcopy(
                lastrows, xe.at[q, pl.ds(0, 16), :], ha_s.at[2], ha_r.at[2 + q], at(prev_i, q)
            ).wait_recv()

    @pl.when(j == NJ - 1)
    def _():
        for q in range(NJ):
            rcopy(
                firstrows, xe.at[q, pl.ds(SR + 48, 16), :], ha_s.at[3], ha_r.at[2 + q],
                at(next_i, q),
            ).wait_recv()

    @pl.when(jnp.logical_and(i == 0, j == 0))
    def _():
        for q in range(NJ):
            xe[q, 0:16, :] = jnp.zeros((16, CW), BF16)

    @pl.when(jnp.logical_and(i == NC - 1, j == NJ - 1))
    def _():
        for q in range(NJ):
            xe[q, SR + 48:SR + 64, :] = jnp.zeros((16, CW), BF16)

    start = pl.multiple_of(SR * j - win(j), 16)

    def slab(k, carry):
        pf, pr = carry

        @pl.when(k > 0)
        def _():
            xa_in(k).wait_recv()

        b = frm(k)
        cols = pl.ds(pl.multiple_of(b * CW, 128), CW)
        cbuf[...] = xe[b, pl.ds(start, SR + 32), :].astype(F32)
        f, r = conv_pair(cw_ref[:, cols], cwr[:, cols])
        flipped = mm(r, anti_b).astype(BF16)
        pf = pf + mm(f, pw_ref[pl.ds(pl.multiple_of(b * CW, 128), CW), :])
        pr = pr + mm(flipped, pw_ref[pl.ds(pl.multiple_of((NJ - 1 - b) * CW, 128), CW), :])
        return pf, pr

    wide = pw_ref.shape[1]
    pf, pr = lax.fori_loop(
        0, NJ, slab, (jnp.zeros((SR, wide), F32), jnp.zeros((SR, wide), F32))
    )
    bc[j, :, 0:2 * N] = pf[:, 0:2 * N].astype(BF16)
    bc[j, :, 2 * N:4 * N] = pr[:, 0:2 * N].astype(BF16)
    heads = HL * NJ
    raw = jnp.concatenate([pf[:, 2 * N:], pr[:, 2 * N:]], axis=1).T
    bias = jnp.concatenate([prm_ref[0], prm_ref[0]], axis=0)
    v = raw + bias
    dts = jnp.maximum(v, 0.0) + jnp.log1p(jnp.exp(-jnp.abs(v)))
    for q in range(NJ):
        dtout[q, 0:HL, :] = dts[q * HL:(q + 1) * HL, :]
        dtout[q, HL:2 * HL, :] = dts[heads + (NJ - 1 - q) * HL:heads + (NJ - q) * HL, :]
    dtin[j] = dtout[j]

    def bcx(k, slot, dev):
        return rcopy(bc.at[slot], bc.at[slot], bc_s.at[k], bc_r.at[k], at(i, dev))

    def dtx(k, slot, dev):
        return rcopy(dtout.at[dev], dtin.at[slot], dt_s.at[k], dt_r.at[k], at(i, dev))

    for k in range(1, NJ):
        dtx(k, j, to(k)).start()
        bcx(k, j, to(k)).start()

    half = pl.ds(pl.multiple_of(core * (CW // 2), 16), CW // 2)

    def wx(k, slot, dev):
        cols = pl.ds(pl.multiple_of((dev // GROUP) * WC, 128), WC)
        return rcopy(
            w_ref.at[half, cols], wbuf.at[slot, half, :], w_s.at[k], w_r.at[k], at(i, dev)
        )

    for k in range(1, NJ):
        wx(k, j, to(k)).start()

    for h in halo:
        h.wait_recv()

    @pl.when(i == 0)
    def _():
        xpad[0:16, :] = jnp.zeros((16, CW), BF16)

    @pl.when(i == NC - 1)
    def _():
        xpad[16 + T:32 + T, :] = jnp.zeros((16, CW), BF16)

    own_conv(0, 0)
    own_conv(NJ - 1, 0)

    own = pl.ds(pl.multiple_of(j * HL, 8), HL)
    mirror = pl.ds(pl.multiple_of((NJ - 1 - j) * HL, 8), HL)

    def own_rows(which):
        return jnp.concatenate([prm_ref[which, own, :], prm_ref[which, mirror, :]], axis=0)

    rate = -jnp.exp(own_rows(1))
    up = jnp.where(iota((SR, SR), 0) <= iota((SR, SR), 1), 1.0, 0.0).astype(F32)
    down = jnp.where(iota((SR, SR), 0) >= iota((SR, SR), 1), 1.0, 0.0).astype(F32)
    is_fwd = iota((2 * HL, SR), 0) < HL

    def states(k, total):
        c = frm(k)

        @pl.when(k > 0)
        def _():
            dtx(k, c, c).wait_recv()
            bcx(k, c, c).wait_recv()

        rows = pl.ds(pl.multiple_of(c * SR, 16), SR)
        dt = dtin[c]
        a = dt * rate
        cum = jnp.where(
            is_fwd,
            mm(a, up, precision=lax.Precision.HIGHEST),
            mm(a, down, precision=lax.Precision.HIGHEST),
        )
        end = jnp.broadcast_to(jnp.sum(a, axis=1, keepdims=True), (2 * HL, SR))
        cumr[c] = cum
        ldr[c] = cum - jnp.log(dt)
        cumc[c] = jnp.concatenate([cum, jnp.zeros((SR - 2 * HL, SR), F32)], axis=0).T
        tail = expand(jnp.exp(end - cum) * dt)
        whole = expand(jnp.exp(end))
        dch[c] = whole[0:8, :]
        tf = (xf[rows, :].astype(F32) * tail[:, 0:CW]).astype(BF16)
        tr = (xr[rows, :].astype(F32) * tail[:, CW:2 * CW]).astype(BF16)
        fresh[c, :, 0:CW] = mm(bc[c, :, 0:N], tf, ((0,), (0,)))
        fresh[c, :, CW:2 * CW] = mm(bc[c, :, 2 * N:3 * N], tr, ((0,), (0,)))
        return total + end

    total = lax.fori_loop(0, NJ, states, jnp.zeros((2 * HL, SR), F32))
    decay_all = expand(jnp.exp(total))[0:8, :]

    stin[...] = jnp.zeros((N, 2 * CW), F32)

    def fold(c, carry):
        r = NJ - 1 - c
        stin[:, 0:CW] = dch[c, 0:1, 0:CW] * stin[:, 0:CW] + fresh[c, :, 0:CW]
        stin[:, CW:2 * CW] = (
            dch[r, 0:1, CW:2 * CW] * stin[:, CW:2 * CW] + fresh[r, :, CW:2 * CW]
        )
        return carry

    lax.fori_loop(0, NJ, fold, 0)

    low4 = iota((8, 128), 0) < 4
    for g in range(N // 8 * HALVES):
        rr, hh = (g // HALVES) * 8, (g % HALVES) * 128
        p, q = g // PP, g % PP
        sxs[p, q, 0:8, :] = stin[rr:rr + 8, hh:hh + 128]
        sxs[p, q, 8:16, :] = stin[rr:rr + 8, CW + hh:CW + hh + 128]
        sxs[p, q, 16:24, :] = jnp.where(
            low4, decay_all[:, hh:hh + 128], decay_all[:, CW + hh:CW + hh + 128]
        )
    sxr[i] = sxs[i]

    def sx(k, slot, dev):
        return rcopy(sxs.at[dev], sxr.at[slot], sx_s.at[k], sx_r.at[k], at(dev, j))

    def sy(k, slot, dev):
        return rcopy(sys_.at[dev], syr.at[slot], sy_s.at[k], sy_r.at[k], at(dev, j))

    def sx_send(k, c):
        sx(k, i, lax.rem(i + k, NC)).start()
        return c

    lax.fori_loop(1, NC, sx_send, 0)

    low = iota((SR, SR), 0) >= iota((SR, SR), 1)
    upp = iota((SR, SR), 0) <= iota((SR, SR), 1)
    lane_head = iota((8, CW), 1) // (CW // HL)
    skips = expand(own_rows(2))[0:8, :]

    def inner(c, carry):
        rows = pl.ds(pl.multiple_of(c * SR, 16), SR)
        cols = cumc[c]
        lds = ldr[c]
        y = jnp.zeros((SR, CW), F32)
        for d, (xs, mask) in enumerate(((xf, low), (xr, upp))):
            xv = xs[rows, :]
            score = mm(bc[c, :, (2 * d + 1) * N:(2 * d + 2) * N], bc[c, :, 2 * d * N:(2 * d + 1) * N], ((1,), (1,)))
            for q in range(HL):
                row = q if d == 0 else 2 * HL - 1 - q
                seg = jnp.where(mask, cols[:, row:row + 1] - lds[row:row + 1, :], -1e30)
                mcat[:, q * SR:(q + 1) * SR] = (score * jnp.exp(seg)).astype(BF16)
                keep = jnp.where(lane_head == q, 1.0, 0.0)[0:1, :].astype(BF16)
                xbd[q * SR:(q + 1) * SR, :] = xv * keep
            y = y + mm(mcat[...], xbd[...])
            y = y + skips[0:1, d * CW:(d + 1) * CW] * xv.astype(F32)
        yacc[rows, :] = y
        return carry

    lax.fori_loop(0, NJ // 2, inner, 0)

    def sx_wait(k, c):
        s = lax.rem(i + NC - k, NC)
        sx(k, s, s).wait_recv()
        return c

    lax.fori_loop(1, NC, sx_wait, 0)

    def link(s, carry):
        ef, eb = carry
        r = NC - 1 - s
        sys_[s, :, 0:8, :] = ef
        sys_[r, :, 8:16, :] = eb
        ef = sxr[s, :, 16:17, :] * ef + sxr[s, :, 0:8, :]
        eb = sxr[r, :, 20:21, :] * eb + sxr[r, :, 8:16, :]
        return ef, eb

    zero = jnp.zeros((PP, 8, 128), F32)
    lax.fori_loop(0, NC, link, (zero, zero))
    syr[i] = sys_[i]

    def sy_send(k, c):
        sy(k, i, lax.rem(i + k, NC)).start()
        return c

    lax.fori_loop(1, NC, sy_send, 0)
    lax.fori_loop(NJ // 2, NJ, inner, 0)

    def sy_wait(k, c):
        s = lax.rem(i + NC - k, NC)
        sy(k, s, s).wait_recv()
        return c

    lax.fori_loop(1, NC, sy_wait, 0)
    for g in range(N // 8 * HALVES):
        rr, hh = (g // HALVES) * 8, (g % HALVES) * 128
        p, q = g // PP, g % PP
        stin[rr:rr + 8, hh:hh + 128] = syr[p, q, 0:8, :]
        stin[rr:rr + 8, CW + hh:CW + hh + 128] = syr[p, q, 8:16, :]

    def finish(s, carry):
        for d in range(2):
            c = s if d == 0 else NJ - 1 - s
            rows = pl.ds(pl.multiple_of(c * SR, 16), SR)
            lanes = slice(d * CW, (d + 1) * CW)
            st = stin[:, lanes]
            z = mm(bc[c, :, (2 * d + 1) * N:(2 * d + 2) * N], st.astype(BF16))
            grown = expand(jnp.exp(cumr[c]))[:, lanes]
            yacc[rows, :] = yacc[rows, :] + grown * z
            stin[:, lanes] = dch[c, 0:1, lanes] * st + fresh[c, :, lanes]
        return carry

    lax.fori_loop(0, NJ, finish, 0)
    comb_s[...] = yacc[...].astype(BF16)

    def cbx(k, slot, dev):
        rows = pl.ds(pl.multiple_of(lax.rem(dev, GROUP) * RB, 16), RB)
        return rcopy(comb_s.at[rows, :], comb_r.at[slot], cb_s.at[k], cb_r.at[k], at(i, dev))

    for k in range(1, NJ):
        cbx(k, j, to(k)).start()
    comb_r[j] = comb_s[pl.ds(pl.multiple_of(yy * RB, 16), RB), :]

    def wfx(k, which):
        s = frm(k)
        part = pl.ds(pl.multiple_of(which * (CW // 2), 16), CW // 2)
        return rcopy(
            wbuf.at[s, part, :], wbuf.at[s, part, :], wf_s.at[k], wf_r.at[k], at(sib, j)
        )

    for k in range(1, NJ):
        wx(k, frm(k), frm(k)).wait_recv()
        wfx(k, core).start()
    for k in range(1, NJ):
        s = frm(k)
        rcopy(gall.at[s], gall.at[s], g_s.at[k], g_r.at[k], at(i, s)).wait_recv()

    acc[...] = jnp.zeros((RB, WC), F32)

    def project(k, squares):
        @pl.when(k > 0)
        def _():
            cbx(k, frm(k), frm(k)).wait_recv()
            wfx(k, 1 - core).wait_recv()

        b = frm(k)
        value = comb_r[b].astype(F32)
        scaled = (value * gall[b, 0:1, :]).astype(BF16)
        acc[...] += mm(scaled, wbuf[b])
        return squares + jnp.sum(value * value, axis=1, keepdims=True)

    squares = lax.fori_loop(0, NJ, project, jnp.zeros((RB, 1), F32))
    scale = lax.rsqrt(squares / D + EPS)
    for q in range(GROUP):
        obs[q] = (acc[:, q * CW:(q + 1) * CW] * scale).astype(BF16)

    def obx(k, slot, dest):
        return rcopy(
            obs.at[dest], obr.at[slot], ob_s.at[k], ob_r.at[k], at(i, xh * GROUP + dest)
        )

    for k in range(1, GROUP):
        obx(k, yy, lax.rem(yy + k, GROUP)).start()
    out_ref[pl.ds(pl.multiple_of(yy * RB, 16), RB), :] = obs[yy]
    for k in range(1, GROUP):
        s = lax.rem(yy + GROUP - k, GROUP)
        obx(k, s, s).wait_recv()
        out_ref[pl.ds(pl.multiple_of(s * RB, 16), RB), :] = obr[s]

    slab_pre.wait_send()
    slab_post.wait_send()
    for h in halo:
        h.wait_send()
    for g in gains:
        g.wait_send()
    for k in range(1, NJ):
        xa(k, to(k)).wait_send()
        dtx(k, j, to(k)).wait_send()
        bcx(k, j, to(k)).wait_send()
        wx(k, j, to(k)).wait_send()
        wfx(k, core).wait_send()
        cbx(k, j, to(k)).wait_send()

    def sent(k, c):
        dev = lax.rem(i + k, NC)
        sx(k, i, dev).wait_send()
        sy(k, i, dev).wait_send()
        return c

    lax.fori_loop(1, NC, sent, 0)
    for k in range(1, GROUP):
        obx(k, yy, lax.rem(yy + k, GROUP)).wait_send()


def shards(x_in, conv_weight, proj_weight, dt_bias, decay_log, skip_gain, norm_gain, out_weight):
    T, CW = x_in.shape
    D = conv_weight.shape[1]
    H = dt_bias.shape[0]
    N = (proj_weight.shape[1] - H) // 2
    NC, NJ = lax.axis_size("ctx"), lax.axis_size("chan")
    HL = H // NJ
    SR = T // NJ
    PP = (N // 8) * (CW // 128) // NC
    RB, WC = T // GROUP, GROUP * CW
    prm = jnp.broadcast_to(jnp.stack([dt_bias, decay_log, skip_gain])[:, :, None], (3, H, 128))
    gain = jnp.broadcast_to(norm_gain[None, :], (8, CW))
    dma = pltpu.SemaphoreType.DMA
    vm = pltpu.VMEM
    scratch = [
        vm((T + 32, CW), BF16), vm((NJ, SR + 64, CW), BF16), vm((SR + 32, CW), F32),
        vm((4, D), F32), vm((T, CW), BF16), vm((T, CW), BF16),
        vm((NJ, SR, 4 * N), BF16), vm((NJ, 2 * HL, SR), F32), vm((NJ, 2 * HL, SR), F32),
        vm((NJ, 2 * HL, SR), F32), vm((NJ, SR, 128), F32), vm((NJ, 2 * HL, SR), F32),
        vm((NJ, N, 2 * CW), F32), vm((NJ, 8, 2 * CW), F32), vm((T, CW), F32),
        vm((SR, HL * SR), BF16), vm((HL * SR, CW), BF16), vm((6 * HL, 2 * CW), BF16),
        vm((NC, PP, 24, 128), F32), vm((NC, PP, 24, 128), F32),
        vm((NC, PP, 16, 128), F32), vm((NC, PP, 16, 128), F32), vm((N, 2 * CW), F32),
        vm((T, CW), BF16), vm((NJ, RB, CW), BF16), vm((NJ, 8, CW), F32),
        vm((NJ, CW, WC), BF16), vm((RB, WC), F32),
        vm((GROUP, RB, CW), BF16), vm((GROUP, RB, CW), BF16),
        dma((NJ,)), dma((NJ,)), dma((4,)), dma((2 + NJ,)), dma((NJ,)), dma((NJ,)),
        dma((NJ,)), dma((NJ,)), dma((NJ,)), dma((NJ,)), dma((NJ,)), dma((NJ,)),
        dma((NJ,)), dma((NJ,)), dma((NC,)), dma((NC,)), dma((NC,)), dma((NC,)),
        dma((NJ,)), dma((NJ,)), dma((GROUP,)), dma((GROUP,)),
    ]
    return pl.pallas_call(
        functools.partial(kernel, (NC, NJ, T, CW, D, N, HL, PP)),
        out_shape=jax.ShapeDtypeStruct((T, CW), BF16),
        in_specs=[pl.BlockSpec(memory_space=pltpu.VMEM)] * 6,
        out_specs=pl.BlockSpec(memory_space=pltpu.VMEM),
        scratch_shapes=scratch,
        compiler_params=pltpu.CompilerParams(
            collective_id=0, has_side_effects=True, vmem_limit_bytes=50 * 1024 * 1024
        ),
        cost_estimate=pl.CostEstimate(
            flops=4 * T * D * CW, bytes_accessed=8 * T * CW, transcendentals=16 * T * SR
        ),
    )(x_in, conv_weight, proj_weight, prm, gain, out_weight)


def solution(mesh):
    in_specs = (P("ctx", "chan"), P(), P(), P(), P(), P(), P("chan"), P("chan", None))
    out_specs = P("ctx", "chan")
    return jax.shard_map(shards, mesh=mesh, in_specs=in_specs, out_specs=out_specs, check_vma=False)
```

time: 743 us -> 110 us (0.15)
  blocking collectives: 260 us -> 0 us
  waiting for transfers between devices: 228 us -> 0 us
  local copies, waits for them, and re-layouts: 137 us -> 3.39 us
  Pallas kernels: 0 us -> 105 us
  matrix products: 46.1 us -> 0 us
  other arithmetic: 38.2 us -> 0.82 us
  starting transfers between devices: 15.1 us -> 0 us
  between operations: 13.8 us -> 0.05 us
    all_to_all x6 -> x0, blocking collectives: 200 us -> none  [the longest x1 77.4 us: mirrored_output(): lax.all_to_all(jnp.flip(block_data, (0, 1)), 'ctx', split_axis=0, concat_...]
    reduce_scatter x1 -> x0, waiting for transfers between devices: 119 us -> none  [shards(): lax.psum_scatter(lax.dot_general(out_weight, normed, (((0,), (1,)), ((),...]
    pallas_call x0 -> x1, Pallas kernels: none -> 105 us  [shards(): pl.pallas_call(functools.partial(kernel, (NC, NJ, T, CW, D, N, HL, PP)),...]
    psum x1 -> x0, waiting for transfers between devices: 58.6 us -> none  [shards(): fwd_proj, rev_proj = lax.psum((fwd_proj, rev_proj), 'chan')]
    dynamic_update_slice x16 -> x0, local copies, waits for them, and re-layouts: 41.7 us -> none  [block_pass(): lax.scan(advance, (start_state, start_offset), (x_blocks, b_blocks, c_blo...]
    dot_general x27 -> x0, matrix products: 39.7 us -> none  [the longest x8 20.4 us: advance(): jnp.einsum('tsh,shp->thp', weights, x_wide, precision=lax.Precision.HIGHEST)]
    all_gather x1 -> x0, blocking collectives: 39.2 us -> none  [carried_in(): gathered = jax.tree.map(lambda a: lax.all_gather(a, axis), part)]
    all_gather x1 -> x0, waiting for transfers between devices: 33.6 us -> none  [carried_in(): gathered = jax.tree.map(lambda a: lax.all_gather(a, axis), part)]
  transfers between devices with their start and end apart: 6 -> 0, of which waited for: 5 -> 0; matrix products, arithmetic and copies ran while one was open for 6% -> 0% of each run, Pallas kernels for 0% -> 0%
where the time goes in v1:
time: 110 us
  Pallas kernels  105 us (95%)
  local copies, waits for them, and re-layouts  3.39 us (3%)
    pallas_call x1, Pallas kernels, shards(): pl.pallas_call(functools.partial(kernel, (NC, NJ, T, CW, D, N, HL, PP)),...  105 us
    unnamed x8, local copies, waits for them, and re-layouts  2.64 us

profile of v1, /device:TPU:1, one launch (start us, length us, event | category | flops | bytes accessed | tf_op | source)
XLA Modules:
  0.0 109.6 jit_solution(5889844696727271264)
XLA Ops:
  0.0 0.0 copy-start
  0.0 0.0 copy-start.2
  0.0 0.0 copy-start.1
  0.0 0.8 pad_maximum_fusion
  0.8 0.7 broadcast_in_dim.5.gain_ref
  1.5 0.1 broadcast_in_dim.4.prm_ref
  1.6 1.8 %copy.9.pw_ref = bf16[2048,320]{1,0:T(8,128)(2,1)S(1)} copy(bf16[2048,320]{0,1:T(8,128)(2,1)} %param.10) | data formatting | bytes 2621440 | tf_op args[2]
  3.4 0.0 copy-done
  3.4 0.0 copy-done.2
  3.4 0.0 copy-done.1
  3.5 105.3 %shard_map.82 = bf16[1024,256]{1,0:T(8,128)(2,1)S(1)} custom-call(bf16[1024,256]{1,0:T(8,128)(2,1)S(1)} %copy-done.1, f32[4,2048]{1,0:T(4,128)S(1)} %copy-done.2, bf16[2048,320]{1,0:T(8,128)(2,1)S(1)} %copy.9.pw_ref, f32[3,64,128]{2,1,0:T(8,128)S(1)} %broadcast_in_dim.4.prm_ref, f32[8,256]{1,0:T(8,128)S(1)} %broadcast_in_dim.5.gain_ref, ...), custom_call_target="tpu_custom_call" | custom-call | flops 2147483648 | bytes 2097152 | tf_op jit(solution)/shard_map/pallas_call | solution.py:535
  108.8 0.8 copy.11
Async XLA Ops:
  0.0 3.4 %copy-start = (bf16[256,2048]{1,0:T(8,128)(2,1)S(1)}, bf16[256,2048]{1,0:T(8,128)(2,1)}, u32[]{:S(2)}) copy-start(bf16[256,2048]{1,0:T(8,128)(2,1)} %w_ref.1) | copy-start | bytes 3145732
  0.0 3.4 %copy-start.2 = (f32[4,2048]{1,0:T(4,128)S(1)}, f32[4,2048]{1,0:T(4,128)}, u32[]{:S(2)}) copy-start(f32[4,2048]{1,0:T(4,128)} %cw_ref.1) | copy-start | bytes 98308
  0.0 3.4 %copy-start.1 = (bf16[1024,256]{1,0:T(8,128)(2,1)S(1)}, bf16[1024,256]{1,0:T(8,128)(2,1)}, u32[]{:S(2)}) copy-start(bf16[1024,256]{1,0:T(8,128)(2,1)} %x_ref.1) | copy-start | bytes 1572868

commit v2 on v1

--- a/solution.py
+++ b/solution.py
@@ -28,11 +28,11 @@
 
 def kernel(
     dims,
-    x_ref, cw_ref, pw_ref, prm_ref, gain_ref, w_ref, out_ref,
-    xpad, xe, cbuf, cwr, xf, xr, bc, dtout, dtin, cumr, cumc, ldr, fresh, dch, yacc,
-    mcat, xbd, emat, sxs, sxr, sys_, syr, stin, comb_s, comb_r, gall, wbuf, acc, obs, obr,
-    xa_s, xa_r, ha_s, ha_r, g_s, g_r, w_s, w_r, wf_s, wf_r, bc_s, bc_r, dt_s, dt_r,
-    sx_s, sx_r, sy_s, sy_r, cb_s, cb_r, ob_s, ob_r,
+    x_ref, cw_ref, pw_ref, bias_ref, decay_ref, skip_ref, gain_ref, w_ref, out_ref,
+    xpad, xe, cbuf, cwr, xf, xr, bb, cc, dtout, dtin, cumr, cumc, ldr, fresh, dch, yacc,
+    mcat, xbd, emat, sxs, sxr, sys_, syr, stin, comb_s, comb_r, gall, wbuf, acc, obs, obr, dec_tile, linked, sqs,
+    xa_s, xa_r, ha_s, ha_r, g_s, g_r, w_s, w_r, wf_s, wf_r, bb_s, bb_r, cc_s, cc_r, dt_s, dt_r,
+    sx_s, sx_r, sy_s, sy_r, cb_s, cb_r, ob_s, ob_r, pwv, pwt, prm, lc,
 ):
     NC, NJ, T, CW, D, N, HL, PP = dims
     SR = T // NJ
@@ -89,10 +89,24 @@
     def win(jd):
         return pl.multiple_of(jnp.clip(SR * jd - 16, 0, T - SR - 32), 16)
 
-    xpad[16:16 + T, :] = x_ref[...]
-    xe[j, 16:SR + 48, :] = x_ref[pl.ds(win(j), SR + 32), :]
-    gall[j] = gain_ref[...]
-    wbuf[j] = w_ref[:, pl.ds(pl.multiple_of(xh * WC, 128), WC)]
+    own_wide = pl.ds(pl.multiple_of(xh * WC, 128), WC)
+    here = [
+        pltpu.make_async_copy(x_ref, xpad.at[pl.ds(16, T), :], lc.at[0]),
+        pltpu.make_async_copy(
+            x_ref.at[pl.ds(win(j), SR + 32), :], xe.at[j, pl.ds(16, SR + 32), :], lc.at[1]
+        ),
+        pltpu.make_async_copy(pw_ref, pwt, lc.at[2]),
+        pltpu.make_async_copy(w_ref.at[:, own_wide], wbuf.at[j], lc.at[3]),
+    ]
+    for h in here:
+        h.start()
+    gall[j] = jnp.broadcast_to(1.0 / (gain_ref[...] * gain_ref[...]), (8, CW))
+    heads = HL * NJ
+    eye = iota((heads, heads), 0) == iota((heads, heads), 1)
+    for q, ref in enumerate((bias_ref, decay_ref, skip_ref)):
+        row = jnp.broadcast_to(ref[...], (heads, heads))
+        column = jnp.sum(jnp.where(eye, row, 0.0), axis=1, keepdims=True)
+        prm[q] = jnp.broadcast_to(column, (heads, 128))
     anti = iota((CW, CW), 0) + iota((CW, CW), 1) == CW - 1
     anti_f = jnp.where(anti, 1.0, 0.0).astype(F32)
     anti_b = anti_f.astype(BF16)
@@ -112,6 +126,10 @@
         mid = rest.astype(BF16)
         low = (rest - mid.astype(F32)).astype(BF16)
         return mm(jnp.concatenate([hi, mid, low], axis=0), emat[...], ((0,), (0,)))
+
+    here[2].wait()
+    for b in range(NJ):
+        pwv[b * CW:(b + 1) * CW, :] = pwt[:, b * CW:(b + 1) * CW].T
 
     pl.semaphore_wait(barrier, NJ - 1 + NC - 1 + 2)
 
@@ -168,6 +186,7 @@
         xr[rows, :] = r
         return carry
 
+    here[0].wait()
     lax.fori_loop(1, NJ - 1, own_conv, 0)
 
     @pl.when(j == 0)
@@ -196,6 +215,7 @@
             xe[q, SR + 48:SR + 64, :] = jnp.zeros((16, CW), BF16)
 
     start = pl.multiple_of(SR * j - win(j), 16)
+    here[1].wait()
 
     def slab(k, carry):
         pf, pr = carry
@@ -209,19 +229,20 @@
         cbuf[...] = xe[b, pl.ds(start, SR + 32), :].astype(F32)
         f, r = conv_pair(cw_ref[:, cols], cwr[:, cols])
         flipped = mm(r, anti_b).astype(BF16)
-        pf = pf + mm(f, pw_ref[pl.ds(pl.multiple_of(b * CW, 128), CW), :])
-        pr = pr + mm(flipped, pw_ref[pl.ds(pl.multiple_of((NJ - 1 - b) * CW, 128), CW), :])
+        pf = pf + mm(f, pwv[pl.ds(pl.multiple_of(b * CW, 128), CW), :])
+        pr = pr + mm(flipped, pwv[pl.ds(pl.multiple_of((NJ - 1 - b) * CW, 128), CW), :])
         return pf, pr
 
-    wide = pw_ref.shape[1]
+    wide = pwv.shape[1]
     pf, pr = lax.fori_loop(
         0, NJ, slab, (jnp.zeros((SR, wide), F32), jnp.zeros((SR, wide), F32))
     )
-    bc[j, :, 0:2 * N] = pf[:, 0:2 * N].astype(BF16)
-    bc[j, :, 2 * N:4 * N] = pr[:, 0:2 * N].astype(BF16)
-    heads = HL * NJ
+    bb[j, :, 0:N] = pf[:, 0:N].astype(BF16)
+    bb[j, :, N:2 * N] = pr[:, 0:N].astype(BF16)
+    cc[j, :, 0:N] = pf[:, N:2 * N].astype(BF16)
+    cc[j, :, N:2 * N] = pr[:, N:2 * N].astype(BF16)
     raw = jnp.concatenate([pf[:, 2 * N:], pr[:, 2 * N:]], axis=1).T
-    bias = jnp.concatenate([prm_ref[0], prm_ref[0]], axis=0)
+    bias = jnp.concatenate([prm[0], prm[0]], axis=0)
     v = raw + bias
     dts = jnp.maximum(v, 0.0) + jnp.log1p(jnp.exp(-jnp.abs(v)))
     for q in range(NJ):
@@ -229,15 +250,18 @@
         dtout[q, HL:2 * HL, :] = dts[heads + (NJ - 1 - q) * HL:heads + (NJ - q) * HL, :]
     dtin[j] = dtout[j]
 
-    def bcx(k, slot, dev):
-        return rcopy(bc.at[slot], bc.at[slot], bc_s.at[k], bc_r.at[k], at(i, dev))
+    def bbx(k, slot, dev):
+        return rcopy(bb.at[slot], bb.at[slot], bb_s.at[k], bb_r.at[k], at(i, dev))
+
+    def ccx(k, slot, dev):
+        return rcopy(cc.at[slot], cc.at[slot], cc_s.at[k], cc_r.at[k], at(i, dev))
 
     def dtx(k, slot, dev):
         return rcopy(dtout.at[dev], dtin.at[slot], dt_s.at[k], dt_r.at[k], at(i, dev))
 
     for k in range(1, NJ):
         dtx(k, j, to(k)).start()
-        bcx(k, j, to(k)).start()
+        bbx(k, j, to(k)).start()
 
     half = pl.ds(pl.multiple_of(core * (CW // 2), 16), CW // 2)
 
@@ -247,9 +271,6 @@
             w_ref.at[half, cols], wbuf.at[slot, half, :], w_s.at[k], w_r.at[k], at(i, dev)
         )
 
-    for k in range(1, NJ):
-        wx(k, j, to(k)).start()
-
     for h in halo:
         h.wait_recv()
 
@@ -268,7 +289,7 @@
     mirror = pl.ds(pl.multiple_of((NJ - 1 - j) * HL, 8), HL)
 
     def own_rows(which):
-        return jnp.concatenate([prm_ref[which, own, :], prm_ref[which, mirror, :]], axis=0)
+        return jnp.concatenate([prm[which, own, :], prm[which, mirror, :]], axis=0)
 
     rate = -jnp.exp(own_rows(1))
     up = jnp.where(iota((SR, SR), 0) <= iota((SR, SR), 1), 1.0, 0.0).astype(F32)
@@ -281,7 +302,8 @@
         @pl.when(k > 0)
         def _():
             dtx(k, c, c).wait_recv()
-            bcx(k, c, c).wait_recv()
+            bbx(k, c, c).wait_recv()
+            ccx(k, j, to(k)).start()
 
         rows = pl.ds(pl.multiple_of(c * SR, 16), SR)
         dt = dtin[c]
@@ -300,12 +322,12 @@
         dch[c] = whole[0:8, :]
         tf = (xf[rows, :].astype(F32) * tail[:, 0:CW]).astype(BF16)
         tr = (xr[rows, :].astype(F32) * tail[:, CW:2 * CW]).astype(BF16)
-        fresh[c, :, 0:CW] = mm(bc[c, :, 0:N], tf, ((0,), (0,)))
-        fresh[c, :, CW:2 * CW] = mm(bc[c, :, 2 * N:3 * N], tr, ((0,), (0,)))
+        fresh[c, :, 0:CW] = mm(bb[c, :, 0:N], tf, ((0,), (0,)))
+        fresh[c, :, CW:2 * CW] = mm(bb[c, :, N:2 * N], tr, ((0,), (0,)))
         return total + end
 
     total = lax.fori_loop(0, NJ, states, jnp.zeros((2 * HL, SR), F32))
-    decay_all = expand(jnp.exp(total))[0:8, :]
+    decay_all = expand(jnp.exp(total))[0:16, :]
 
     stin[...] = jnp.zeros((N, 2 * CW), F32)
 
@@ -319,15 +341,26 @@
 
     lax.fori_loop(0, NJ, fold, 0)
 
-    low4 = iota((8, 128), 0) < 4
+    place = iota((16, 128), 0)
+    ahead = lax.rem(place, 4) < 2
     for g in range(N // 8 * HALVES):
         rr, hh = (g // HALVES) * 8, (g % HALVES) * 128
         p, q = g // PP, g % PP
-        sxs[p, q, 0:8, :] = stin[rr:rr + 8, hh:hh + 128]
-        sxs[p, q, 8:16, :] = stin[rr:rr + 8, CW + hh:CW + hh + 128]
-        sxs[p, q, 16:24, :] = jnp.where(
-            low4, decay_all[:, hh:hh + 128], decay_all[:, CW + hh:CW + hh + 128]
-        )
+        both = jnp.concatenate(
+            [stin[rr:rr + 8, hh:hh + 128], stin[rr:rr + 8, CW + hh:CW + hh + 128]], axis=0
+        )
+        sxs[p, q, 0:16, :] = both.astype(BF16)
+        if rr == 0:
+            dec = jnp.where(
+                ahead, decay_all[:, hh:hh + 128], decay_all[:, CW + hh:CW + hh + 128]
+            )
+            first = dec.astype(BF16).astype(F32)
+            second = (dec - first).astype(BF16).astype(F32)
+            third = dec - first - second
+            dec_tile[hh // 128] = jnp.where(
+                place < 4, first, jnp.where(place < 8, second, third)
+            ).astype(BF16)
+        sxs[p, q, 16:32, :] = dec_tile[hh // 128]
     sxr[i] = sxs[i]
 
     def sx(k, slot, dev):
@@ -347,14 +380,29 @@
     lane_head = iota((8, CW), 1) // (CW // HL)
     skips = expand(own_rows(2))[0:8, :]
 
-    def inner(c, carry):
+    def inner(k, carry):
+        c = frm(k)
+
+        @pl.when(k > 0)
+        def _():
+            ccx(k, c, c).wait_recv()
+
+            @pl.when(k < NJ // 2)
+            def _():
+                wx(2 * k, j, to(2 * k)).start()
+
+        @pl.when(k < NJ // 2)
+        def _():
+            wx(2 * k + 1, j, to(2 * k + 1)).start()
+
         rows = pl.ds(pl.multiple_of(c * SR, 16), SR)
         cols = cumc[c]
         lds = ldr[c]
         y = jnp.zeros((SR, CW), F32)
         for d, (xs, mask) in enumerate(((xf, low), (xr, upp))):
             xv = xs[rows, :]
-            score = mm(bc[c, :, (2 * d + 1) * N:(2 * d + 2) * N], bc[c, :, 2 * d * N:(2 * d + 1) * N], ((1,), (1,)))
+            part = slice(d * N, (d + 1) * N)
+            score = mm(cc[c, :, part], bb[c, :, part], ((1,), (1,)))
             for q in range(HL):
                 row = q if d == 0 else 2 * HL - 1 - q
                 seg = jnp.where(mask, cols[:, row:row + 1] - lds[row:row + 1, :], -1e30)
@@ -378,14 +426,18 @@
     def link(s, carry):
         ef, eb = carry
         r = NC - 1 - s
-        sys_[s, :, 0:8, :] = ef
-        sys_[r, :, 8:16, :] = eb
-        ef = sxr[s, :, 16:17, :] * ef + sxr[s, :, 0:8, :]
-        eb = sxr[r, :, 20:21, :] * eb + sxr[r, :, 8:16, :]
+        linked[s, :, 0:8, :] = ef
+        linked[r, :, 8:16, :] = eb
+        vf, vb = sxr[s].astype(F32), sxr[r].astype(F32)
+        df = vf[:, 16:17, :] + vf[:, 20:21, :] + vf[:, 24:25, :]
+        db = vb[:, 18:19, :] + vb[:, 22:23, :] + vb[:, 26:27, :]
+        ef = df * ef + vf[:, 0:8, :]
+        eb = db * eb + vb[:, 8:16, :]
         return ef, eb
 
     zero = jnp.zeros((PP, 8, 128), F32)
     lax.fori_loop(0, NC, link, (zero, zero))
+    sys_[...] = linked[...].astype(BF16)
     syr[i] = sys_[i]
 
     def sy_send(k, c):
@@ -404,8 +456,9 @@
     for g in range(N // 8 * HALVES):
         rr, hh = (g // HALVES) * 8, (g % HALVES) * 128
         p, q = g // PP, g % PP
-        stin[rr:rr + 8, hh:hh + 128] = syr[p, q, 0:8, :]
-        stin[rr:rr + 8, CW + hh:CW + hh + 128] = syr[p, q, 8:16, :]
+        piece = syr[p, q].astype(F32)
+        stin[rr:rr + 8, hh:hh + 128] = piece[0:8]
+        stin[rr:rr + 8, CW + hh:CW + hh + 128] = piece[8:16]
 
     def finish(s, carry):
         for d in range(2):
@@ -413,14 +466,14 @@
             rows = pl.ds(pl.multiple_of(c * SR, 16), SR)
             lanes = slice(d * CW, (d + 1) * CW)
             st = stin[:, lanes]
-            z = mm(bc[c, :, (2 * d + 1) * N:(2 * d + 2) * N], st.astype(BF16))
+            z = mm(cc[c, :, d * N:(d + 1) * N], st.astype(BF16))
             grown = expand(jnp.exp(cumr[c]))[:, lanes]
             yacc[rows, :] = yacc[rows, :] + grown * z
             stin[:, lanes] = dch[c, 0:1, lanes] * st + fresh[c, :, lanes]
         return carry
 
     lax.fori_loop(0, NJ, finish, 0)
-    comb_s[...] = yacc[...].astype(BF16)
+    comb_s[...] = (yacc[...] * gain_ref[...]).astype(BF16)
 
     def cbx(k, slot, dev):
         rows = pl.ds(pl.multiple_of(lax.rem(dev, GROUP) * RB, 16), RB)
@@ -445,21 +498,23 @@
         rcopy(gall.at[s], gall.at[s], g_s.at[k], g_r.at[k], at(i, s)).wait_recv()
 
     acc[...] = jnp.zeros((RB, WC), F32)
-
-    def project(k, squares):
+    here[3].wait()
+
+    def project(k, carry):
         @pl.when(k > 0)
         def _():
             cbx(k, frm(k), frm(k)).wait_recv()
             wfx(k, 1 - core).wait_recv()
 
         b = frm(k)
+        acc[...] += mm(comb_r[b], wbuf[b])
         value = comb_r[b].astype(F32)
-        scaled = (value * gall[b, 0:1, :]).astype(BF16)
-        acc[...] += mm(scaled, wbuf[b])
-        return squares + jnp.sum(value * value, axis=1, keepdims=True)
-
-    squares = lax.fori_loop(0, NJ, project, jnp.zeros((RB, 1), F32))
-    scale = lax.rsqrt(squares / D + EPS)
+        sqs[...] += value * value * gall[b, 0:1, :]
+        return carry
+
+    sqs[...] = jnp.zeros((RB, CW), F32)
+    lax.fori_loop(0, NJ, project, 0)
+    scale = lax.rsqrt(jnp.sum(sqs[...], axis=1, keepdims=True) / D + EPS)
     for q in range(GROUP):
         obs[q] = (acc[:, q * CW:(q + 1) * CW] * scale).astype(BF16)
 
@@ -485,7 +540,8 @@
     for k in range(1, NJ):
         xa(k, to(k)).wait_send()
         dtx(k, j, to(k)).wait_send()
-        bcx(k, j, to(k)).wait_send()
+        bbx(k, j, to(k)).wait_send()
+        ccx(k, j, to(k)).wait_send()
         wx(k, j, to(k)).wait_send()
         wfx(k, core).wait_send()
         cbx(k, j, to(k)).wait_send()
@@ -511,40 +567,47 @@
     SR = T // NJ
     PP = (N // 8) * (CW // 128) // NC
     RB, WC = T // GROUP, GROUP * CW
-    prm = jnp.broadcast_to(jnp.stack([dt_bias, decay_log, skip_gain])[:, :, None], (3, H, 128))
-    gain = jnp.broadcast_to(norm_gain[None, :], (8, CW))
     dma = pltpu.SemaphoreType.DMA
     vm = pltpu.VMEM
     scratch = [
         vm((T + 32, CW), BF16), vm((NJ, SR + 64, CW), BF16), vm((SR + 32, CW), F32),
         vm((4, D), F32), vm((T, CW), BF16), vm((T, CW), BF16),
-        vm((NJ, SR, 4 * N), BF16), vm((NJ, 2 * HL, SR), F32), vm((NJ, 2 * HL, SR), F32),
+        vm((NJ, SR, 2 * N), BF16), vm((NJ, SR, 2 * N), BF16),
+        vm((NJ, 2 * HL, SR), F32), vm((NJ, 2 * HL, SR), F32),
         vm((NJ, 2 * HL, SR), F32), vm((NJ, SR, 128), F32), vm((NJ, 2 * HL, SR), F32),
         vm((NJ, N, 2 * CW), F32), vm((NJ, 8, 2 * CW), F32), vm((T, CW), F32),
         vm((SR, HL * SR), BF16), vm((HL * SR, CW), BF16), vm((6 * HL, 2 * CW), BF16),
-        vm((NC, PP, 24, 128), F32), vm((NC, PP, 24, 128), F32),
-        vm((NC, PP, 16, 128), F32), vm((NC, PP, 16, 128), F32), vm((N, 2 * CW), F32),
+        vm((NC, PP, 32, 128), BF16), vm((NC, PP, 32, 128), BF16),
+        vm((NC, PP, 16, 128), BF16), vm((NC, PP, 16, 128), BF16), vm((N, 2 * CW), F32),
         vm((T, CW), BF16), vm((NJ, RB, CW), BF16), vm((NJ, 8, CW), F32),
         vm((NJ, CW, WC), BF16), vm((RB, WC), F32),
         vm((GROUP, RB, CW), BF16), vm((GROUP, RB, CW), BF16),
+        vm((CW // 128, 16, 128), BF16), vm((NC, PP, 16, 128), F32), vm((RB, CW), F32),
         dma((NJ,)), dma((NJ,)), dma((4,)), dma((2 + NJ,)), dma((NJ,)), dma((NJ,)),
         dma((NJ,)), dma((NJ,)), dma((NJ,)), dma((NJ,)), dma((NJ,)), dma((NJ,)),
-        dma((NJ,)), dma((NJ,)), dma((NC,)), dma((NC,)), dma((NC,)), dma((NC,)),
+        dma((NJ,)), dma((NJ,)), dma((NJ,)), dma((NJ,)),
+        dma((NC,)), dma((NC,)), dma((NC,)), dma((NC,)),
         dma((NJ,)), dma((NJ,)), dma((GROUP,)), dma((GROUP,)),
+        vm(proj_weight.shape, BF16), vm(proj_weight.shape[::-1], BF16), vm((3, H, 128), F32), dma((4,)),
     ]
     return pl.pallas_call(
         functools.partial(kernel, (NC, NJ, T, CW, D, N, HL, PP)),
         out_shape=jax.ShapeDtypeStruct((T, CW), BF16),
-        in_specs=[pl.BlockSpec(memory_space=pltpu.VMEM)] * 6,
+        in_specs=[
+            pl.BlockSpec(memory_space=pl.ANY if q in (0, 2, 7) else pltpu.VMEM) for q in range(8)
+        ],
         out_specs=pl.BlockSpec(memory_space=pltpu.VMEM),
         scratch_shapes=scratch,
         compiler_params=pltpu.CompilerParams(
-            collective_id=0, has_side_effects=True, vmem_limit_bytes=50 * 1024 * 1024
+            collective_id=0, has_side_effects=True, vmem_limit_bytes=62 * 1024 * 1024
         ),
         cost_estimate=pl.CostEstimate(
             flops=4 * T * D * CW, bytes_accessed=8 * T * CW, transcendentals=16 * T * SR
         ),
-    )(x_in, conv_weight, proj_weight, prm, gain, out_weight)
+    )(
+        x_in, conv_weight, proj_weight.T, dt_bias[None], decay_log[None], skip_gain[None],
+        norm_gain[None], out_weight,
+    )
 
 
 def solution(mesh):

time: 110 us -> 102 us (0.927)
  Pallas kernels: 105 us -> 98.8 us
  local copies, waits for them, and re-layouts: 3.39 us -> 1.87 us
    pallas_call x1, Pallas kernels: 105 us -> 98.8 us  [shards(): pl.pallas_call(functools.partial(kernel, (NC, NJ, T, CW, D, N, HL, PP)),...]
    unnamed x8 -> x1, local copies, waits for them, and re-layouts: 2.64 us -> 1.87 us
where the time goes in v2:
time: 102 us; the launch traced here: 101 us
  Pallas kernels  98.8 us (97%)
  local copies, waits for them, and re-layouts  1.87 us (2%)
    pallas_call x1, Pallas kernels, shards(): pl.pallas_call(functools.partial(kernel, (NC, NJ, T, CW, D, N, HL, PP)),...  98.8 us

profile of v2, /device:TPU:1, one launch (start us, length us, event | category | flops | bytes accessed | tf_op | source)
XLA Modules:
  0.0 100.7 jit_solution(11616223103635350945)
XLA Ops:
  0.0 98.8 %shard_map.82 = bf16[1024,256]{1,0:T(8,128)(2,1)} custom-call(bf16[1024,256]{1,0:T(8,128)(2,1)} %x_ref.1, f32[4,2048]{1,0:T(4,128)} %cw_ref.1, bf16[320,2048]{1,0:T(8,128)(2,1)} %bitcast.5, f32[1,64]{1,0:T(1,128)} %bitcast.7, f32[1,64]{1,0:T(1,128)} %bitcast.8, f32[1,64]{1,0:T(1,128)} %bitcast.9, f32[1,256]{1,0:T(1,128)} %bitcast.6, bf16[256,2048]{1,0:T(8,128)(2,1)} %w_ref.1), custom_call_target="tpu_custom_call" | custom-call | flops 2147483648 | bytes 2097152 | tf_op jit(solution)/shard_map/pallas_call | solution.py:593
  98.8 1.9 %copy.10 = bf16[1024,256]{1,0:T(8,128)(2,1)} copy(bf16[1024,256]{1,0:T(8,128)(2,1)} %shard_map.82) | data formatting | bytes 1048576

commit v3 on v2

--- a/solution.py
+++ b/solution.py
@@ -30,13 +30,15 @@
     dims,
     x_ref, cw_ref, pw_ref, bias_ref, decay_ref, skip_ref, gain_ref, w_ref, out_ref,
     xpad, xe, cbuf, cwr, xf, xr, bb, cc, dtout, dtin, cumr, cumc, ldr, fresh, dch, yacc,
-    mcat, xbd, emat, sxs, sxr, sys_, syr, stin, comb_s, comb_r, gall, wbuf, acc, obs, obr, dec_tile, linked, sqs,
-    xa_s, xa_r, ha_s, ha_r, g_s, g_r, w_s, w_r, wf_s, wf_r, bb_s, bb_r, cc_s, cc_r, dt_s, dt_r,
-    sx_s, sx_r, sy_s, sy_r, cb_s, cb_r, ob_s, ob_r, pwv, pwt, prm, lc,
+    mcat, xbd, emat, zs, zr, es, er, xs_, xr_, st_o, ech, dec_me, dec_o, stin, comb_s, comb_r, gall, wbuf, acc, obs, obr, sqs,
+    xa_s, xa_r, ha_s, ha_r, g_s, g_r, w_s, w_r, up_s, up_r, dn_s, dn_r, bb_s, bb_r, cc_s, cc_r, dt_s, dt_r,
+    zx_s, zx_r, zy_s, zy_r, sb_s, sb_r, cb_s, cb_r, ob_s, ob_r, pwv, pwt, prm, lc,
 ):
-    NC, NJ, T, CW, D, N, HL, PP = dims
+    NC, NJ, T, CW, D, N, HL, XL, ZC = dims
     SR = T // NJ
-    HALVES = CW // 128
+    PR = N // 2 // ZC
+    LB = 2 * CW // 128
+    WR = CW // 2 // ZC
     RB = T // GROUP
     WC = GROUP * CW
     i = lax.axis_index("ctx")
@@ -45,6 +47,8 @@
     next_i = lax.rem(i + 1, NC)
     core = lax.rem(i, 2)
     sib = i + 1 - 2 * core
+    xlo = i // (2 * ZC)
+    zi = lax.rem(i // 2, ZC)
     xh = j // GROUP
     yy = lax.rem(j, GROUP)
 
@@ -70,11 +74,22 @@
     for k in range(1, NJ):
         hail(at(i, to(k)))
 
-    def hail_ctx(k, c):
-        hail(at(lax.rem(i + k, NC), j))
-        return c
-
-    lax.fori_loop(1, NC, hail_ctx, 0)
+    def zpos(z):
+        return xlo * (2 * ZC) + z * 2 + core
+
+    def zto(k):
+        return lax.rem(zi + k, ZC)
+
+    def zfrm(k):
+        return lax.rem(zi + ZC - k, ZC)
+
+    for k in range(1, ZC):
+        hail(at(zpos(zto(k)), j))
+    across = lax.rem(i + 2 * ZC, NC)
+    if XL > 1:
+        hail(at(across, j))
+    for c in (sib, prev_i, next_i):
+        hail(at(c, j))
 
     @pl.when(j == 0)
     def _():
@@ -88,6 +103,9 @@
 
     def win(jd):
         return pl.multiple_of(jnp.clip(SR * jd - 16, 0, T - SR - 32), 16)
+
+    def wrows(z):
+        return pl.ds(pl.multiple_of(core * (CW // 2) + z * WR, 16), WR)
 
     own_wide = pl.ds(pl.multiple_of(xh * WC, 128), WC)
     here = [
@@ -96,7 +114,9 @@
             x_ref.at[pl.ds(win(j), SR + 32), :], xe.at[j, pl.ds(16, SR + 32), :], lc.at[1]
         ),
         pltpu.make_async_copy(pw_ref, pwt, lc.at[2]),
-        pltpu.make_async_copy(w_ref.at[:, own_wide], wbuf.at[j], lc.at[3]),
+        pltpu.make_async_copy(
+            w_ref.at[wrows(zi), own_wide], wbuf.at[j, wrows(zi), :], lc.at[3]
+        ),
     ]
     for h in here:
         h.start()
@@ -114,11 +134,11 @@
         cwr[:, b * CW:(b + 1) * CW] = mm(
             cw_ref[:, (NJ - 1 - b) * CW:(NJ - b) * CW], anti_f, precision=lax.Precision.HIGHEST
         )
-    er = lax.rem(iota((6 * HL, 2 * CW), 0), 2 * HL)
+    head_row = lax.rem(iota((6 * HL, 2 * CW), 0), 2 * HL)
     ec = iota((6 * HL, 2 * CW), 1)
     head_of = ec // (CW // HL)
     target = jnp.where(head_of < HL, head_of, 3 * HL - 1 - head_of)
-    emat[...] = jnp.where(er == target, 1.0, 0.0).astype(BF16)
+    emat[...] = jnp.where(head_row == target, 1.0, 0.0).astype(BF16)
 
     def expand(rows):
         hi = rows.astype(BF16)
@@ -131,7 +151,7 @@
     for b in range(NJ):
         pwv[b * CW:(b + 1) * CW, :] = pwt[:, b * CW:(b + 1) * CW].T
 
-    pl.semaphore_wait(barrier, NJ - 1 + NC - 1 + 2)
+    pl.semaphore_wait(barrier, NJ - 1 + ZC - 1 + XL - 1 + 3 + 2)
 
     def xa(k, jd):
         return rcopy(
@@ -217,8 +237,40 @@
     start = pl.multiple_of(SR * j - win(j), 16)
     here[1].wait()
 
+    def wx(k, slot, dev):
+        cols = pl.ds(pl.multiple_of((dev // GROUP) * WC, 128), WC)
+        return rcopy(
+            w_ref.at[wrows(zi), cols], wbuf.at[slot, wrows(zi), :], w_s.at[k], w_r.at[k],
+            at(i, dev),
+        )
+
+    def up_ring(d, z):
+        part = wbuf.at[:, wrows(z), :]
+        return rcopy(part, part, up_s.at[d], up_r.at[d], at(zpos(zto(1)), j))
+
+    def down_ring(d, z):
+        part = wbuf.at[:, wrows(z), :]
+        return rcopy(part, part, dn_s.at[d], dn_r.at[d], at(zpos(zfrm(1)), j))
+
+    def ring_start(d):
+        if d < ZC // 2:
+            up_ring(d, zfrm(d)).start()
+        if d < (ZC - 1) // 2:
+            down_ring(d, zto(d)).start()
+
+    def ring_wait(d):
+        if d < ZC // 2:
+            up_ring(d, zfrm(d + 1)).wait_recv()
+        if d < (ZC - 1) // 2:
+            down_ring(d, zto(d + 1)).wait_recv()
+
     def slab(k, carry):
         pf, pr = carry
+
+        @pl.when(k == NJ // 2)
+        def _():
+            for q in range(1, NJ):
+                wx(q, j, to(q)).start()
 
         @pl.when(k > 0)
         def _():
@@ -263,13 +315,10 @@
         dtx(k, j, to(k)).start()
         bbx(k, j, to(k)).start()
 
-    half = pl.ds(pl.multiple_of(core * (CW // 2), 16), CW // 2)
-
-    def wx(k, slot, dev):
-        cols = pl.ds(pl.multiple_of((dev // GROUP) * WC, 128), WC)
-        return rcopy(
-            w_ref.at[half, cols], wbuf.at[slot, half, :], w_s.at[k], w_r.at[k], at(i, dev)
-        )
+    for k in range(1, NJ):
+        wx(k, frm(k), frm(k)).wait_recv()
+    here[3].wait()
+    ring_start(0)
 
     for h in halo:
         h.wait_recv()
@@ -327,7 +376,7 @@
         return total + end
 
     total = lax.fori_loop(0, NJ, states, jnp.zeros((2 * HL, SR), F32))
-    decay_all = expand(jnp.exp(total))[0:16, :]
+    dec_me[...] = expand(jnp.exp(total))[0:8, :]
 
     stin[...] = jnp.zeros((N, 2 * CW), F32)
 
@@ -341,39 +390,41 @@
 
     lax.fori_loop(0, NJ, fold, 0)
 
-    place = iota((16, 128), 0)
-    ahead = lax.rem(place, 4) < 2
-    for g in range(N // 8 * HALVES):
-        rr, hh = (g // HALVES) * 8, (g % HALVES) * 128
-        p, q = g // PP, g % PP
-        both = jnp.concatenate(
-            [stin[rr:rr + 8, hh:hh + 128], stin[rr:rr + 8, CW + hh:CW + hh + 128]], axis=0
-        )
-        sxs[p, q, 0:16, :] = both.astype(BF16)
-        if rr == 0:
-            dec = jnp.where(
-                ahead, decay_all[:, hh:hh + 128], decay_all[:, CW + hh:CW + hh + 128]
-            )
-            first = dec.astype(BF16).astype(F32)
-            second = (dec - first).astype(BF16).astype(F32)
-            third = dec - first - second
-            dec_tile[hh // 128] = jnp.where(
-                place < 4, first, jnp.where(place < 8, second, third)
-            ).astype(BF16)
-        sxs[p, q, 16:32, :] = dec_tile[hh // 128]
-    sxr[i] = sxs[i]
-
-    def sx(k, slot, dev):
-        return rcopy(sxs.at[dev], sxr.at[slot], sx_s.at[k], sx_r.at[k], at(dev, j))
-
-    def sy(k, slot, dev):
-        return rcopy(sys_.at[dev], syr.at[slot], sy_s.at[k], sy_r.at[k], at(dev, j))
-
-    def sx_send(k, c):
-        sx(k, i, lax.rem(i + k, NC)).start()
-        return c
-
-    lax.fori_loop(1, NC, sx_send, 0)
+    swap = [
+        rcopy(stin, st_o, sb_s.at[0], sb_r.at[0], at(sib, j)),
+        rcopy(dec_me, dec_o, sb_s.at[1], sb_r.at[1], at(sib, j)),
+    ]
+    for h in swap:
+        h.start()
+    ring_wait(0)
+    ring_start(1)
+    for h in swap:
+        h.wait_recv()
+    mine = pl.ds(pl.multiple_of(core * (N // 2), 8), N // 2)
+    s_me, s_o = stin[mine, :], st_o[mine, :]
+    d_me, d_o = dec_me[0:1, :], dec_o[0:1, :]
+    fwd_lane = jnp.where(iota((8, 2 * CW), 1) < CW, 1, 0)[0:1, :]
+    other_last = fwd_lane == 1 - core
+    pair = jnp.where(other_last, d_o * s_me + s_o, d_me * s_o + s_me)
+    d_pair = jnp.broadcast_to(d_me * d_o, (8, 2 * CW))
+    place = iota((8, 128), 0)
+    d_tile = jnp.zeros((8, 128), F32)
+    for q in range(LB):
+        d_tile = jnp.where(place == q, d_pair[:, q * 128:(q + 1) * 128], d_tile)
+    for p in range(ZC):
+        for q in range(LB):
+            zs[p, q * PR:(q + 1) * PR, :] = pair[p * PR:(p + 1) * PR, q * 128:(q + 1) * 128]
+        zs[p, LB * PR:LB * PR + 8, :] = d_tile
+    zr[zi] = zs[zi]
+
+    def zx(k, slot, z):
+        return rcopy(zs.at[z], zr.at[slot], zx_s.at[k], zx_r.at[k], at(zpos(z), j))
+
+    def zy(k, slot, z):
+        return rcopy(es.at[z], er.at[slot], zy_s.at[k], zy_r.at[k], at(zpos(z), j))
+
+    for k in range(1, ZC):
+        zx(k, zi, zto(k)).start()
 
     low = iota((SR, SR), 0) >= iota((SR, SR), 1)
     upp = iota((SR, SR), 0) <= iota((SR, SR), 1)
@@ -386,14 +437,6 @@
         @pl.when(k > 0)
         def _():
             ccx(k, c, c).wait_recv()
-
-            @pl.when(k < NJ // 2)
-            def _():
-                wx(2 * k, j, to(2 * k)).start()
-
-        @pl.when(k < NJ // 2)
-        def _():
-            wx(2 * k + 1, j, to(2 * k + 1)).start()
 
         rows = pl.ds(pl.multiple_of(c * SR, 16), SR)
         cols = cumc[c]
@@ -414,51 +457,57 @@
         yacc[rows, :] = y
         return carry
 
-    lax.fori_loop(0, NJ // 2, inner, 0)
-
-    def sx_wait(k, c):
-        s = lax.rem(i + NC - k, NC)
-        sx(k, s, s).wait_recv()
-        return c
-
-    lax.fori_loop(1, NC, sx_wait, 0)
-
-    def link(s, carry):
-        ef, eb = carry
-        r = NC - 1 - s
-        linked[s, :, 0:8, :] = ef
-        linked[r, :, 8:16, :] = eb
-        vf, vb = sxr[s].astype(F32), sxr[r].astype(F32)
-        df = vf[:, 16:17, :] + vf[:, 20:21, :] + vf[:, 24:25, :]
-        db = vb[:, 18:19, :] + vb[:, 22:23, :] + vb[:, 26:27, :]
-        ef = df * ef + vf[:, 0:8, :]
-        eb = db * eb + vb[:, 8:16, :]
-        return ef, eb
-
-    zero = jnp.zeros((PP, 8, 128), F32)
-    lax.fori_loop(0, NC, link, (zero, zero))
-    sys_[...] = linked[...].astype(BF16)
-    syr[i] = sys_[i]
-
-    def sy_send(k, c):
-        sy(k, i, lax.rem(i + k, NC)).start()
-        return c
-
-    lax.fori_loop(1, NC, sy_send, 0)
-    lax.fori_loop(NJ // 2, NJ, inner, 0)
-
-    def sy_wait(k, c):
-        s = lax.rem(i + NC - k, NC)
-        sy(k, s, s).wait_recv()
-        return c
-
-    lax.fori_loop(1, NC, sy_wait, 0)
-    for g in range(N // 8 * HALVES):
-        rr, hh = (g // HALVES) * 8, (g % HALVES) * 128
-        p, q = g // PP, g % PP
-        piece = syr[p, q].astype(F32)
-        stin[rr:rr + 8, hh:hh + 128] = piece[0:8]
-        stin[rr:rr + 8, CW + hh:CW + hh + 128] = piece[8:16]
+    lax.fori_loop(0, 3, inner, 0)
+
+    ring_wait(1)
+    ring_start(2)
+    for k in range(1, ZC):
+        zx(k, zfrm(k), zfrm(k)).wait_recv()
+
+    def chain(q, e, keep):
+        order = range(ZC) if q < LB // 2 else range(ZC - 1, -1, -1)
+        rows = slice(q * PR, (q + 1) * PR)
+        for z in order:
+            if keep:
+                es[z, rows, :] = e
+            e = zr[z, LB * PR + q:LB * PR + q + 1, :] * e + zr[z, rows, :]
+        return e
+
+    zero = jnp.zeros((PR, 128), F32)
+    if XL > 1:
+        for q in range(LB):
+            xs_[q * PR:(q + 1) * PR, :] = chain(q, zero, False)
+        cross = rcopy(xs_, xr_, sb_s.at[2], sb_r.at[2], at(across, j))
+        cross.start()
+        lax.fori_loop(3, 4, inner, 0)
+        cross.wait_recv()
+    for q in range(LB):
+        start_from = zero
+        if XL > 1:
+            takes = xlo == 1 if q < LB // 2 else xlo == 0
+            start_from = jnp.where(takes, xr_[q * PR:(q + 1) * PR, :], 0.0)
+        chain(q, start_from, True)
+    er[zi] = es[zi]
+    for k in range(1, ZC):
+        zy(k, zi, zto(k)).start()
+    lax.fori_loop(4 if XL > 1 else 3, NJ, inner, 0)
+    ring_wait(2)
+    ring_start(3)
+    for k in range(1, ZC):
+        zy(k, zfrm(k), zfrm(k)).wait_recv()
+    for p in range(ZC):
+        for q in range(LB):
+            ech[pl.ds(pl.multiple_of(core * (N // 2) + p * PR, 8), PR), q * 128:(q + 1) * 128] = (
+                er[p, q * PR:(q + 1) * PR, :]
+            )
+    halves = rcopy(ech.at[mine, :], ech.at[mine, :], sb_s.at[3], sb_r.at[3], at(sib, j))
+    halves.start()
+    for h in swap:
+        h.wait_send()
+    theirs = pl.ds(pl.multiple_of((1 - core) * (N // 2), 8), N // 2)
+    rcopy(ech.at[theirs, :], ech.at[theirs, :], sb_s.at[3], sb_r.at[3], at(sib, j)).wait_recv()
+    other_first = fwd_lane == core
+    stin[...] = jnp.where(other_first, dec_o[0:1, :] * ech[...] + st_o[...], ech[...])
 
     def finish(s, carry):
         for d in range(2):
@@ -483,28 +532,24 @@
         cbx(k, j, to(k)).start()
     comb_r[j] = comb_s[pl.ds(pl.multiple_of(yy * RB, 16), RB), :]
 
-    def wfx(k, which):
-        s = frm(k)
-        part = pl.ds(pl.multiple_of(which * (CW // 2), 16), CW // 2)
-        return rcopy(
-            wbuf.at[s, part, :], wbuf.at[s, part, :], wf_s.at[k], wf_r.at[k], at(sib, j)
-        )
-
-    for k in range(1, NJ):
-        wx(k, frm(k), frm(k)).wait_recv()
-        wfx(k, core).start()
+    ring_wait(3)
+    half = pl.ds(pl.multiple_of(core * (CW // 2), 16), CW // 2)
+    rest = pl.ds(pl.multiple_of((1 - core) * (CW // 2), 16), CW // 2)
+    share = rcopy(wbuf.at[:, half, :], wbuf.at[:, half, :], sb_s.at[4], sb_r.at[4], at(sib, j))
+    share.start()
     for k in range(1, NJ):
         s = frm(k)
         rcopy(gall.at[s], gall.at[s], g_s.at[k], g_r.at[k], at(i, s)).wait_recv()
 
     acc[...] = jnp.zeros((RB, WC), F32)
-    here[3].wait()
+    rcopy(
+        wbuf.at[:, rest, :], wbuf.at[:, rest, :], sb_s.at[4], sb_r.at[4], at(sib, j)
+    ).wait_recv()
 
     def project(k, carry):
         @pl.when(k > 0)
         def _():
             cbx(k, frm(k), frm(k)).wait_recv()
-            wfx(k, 1 - core).wait_recv()
 
         b = frm(k)
         acc[...] += mm(comb_r[b], wbuf[b])
@@ -543,16 +588,19 @@
         bbx(k, j, to(k)).wait_send()
         ccx(k, j, to(k)).wait_send()
         wx(k, j, to(k)).wait_send()
-        wfx(k, core).wait_send()
         cbx(k, j, to(k)).wait_send()
 
-    def sent(k, c):
-        dev = lax.rem(i + k, NC)
-        sx(k, i, dev).wait_send()
-        sy(k, i, dev).wait_send()
-        return c
-
-    lax.fori_loop(1, NC, sent, 0)
+    for k in range(1, ZC):
+        zx(k, zi, zto(k)).wait_send()
+        zy(k, zi, zto(k)).wait_send()
+    if XL > 1:
+        cross.wait_send()
+    halves.wait_send()
+    share.wait_send()
+    for d in range(ZC // 2):
+        up_ring(d, zfrm(d)).wait_send()
+    for d in range((ZC - 1) // 2):
+        down_ring(d, zto(d)).wait_send()
     for k in range(1, GROUP):
         obx(k, yy, lax.rem(yy + k, GROUP)).wait_send()
 
@@ -565,7 +613,9 @@
     NC, NJ = lax.axis_size("ctx"), lax.axis_size("chan")
     HL = H // NJ
     SR = T // NJ
-    PP = (N // 8) * (CW // 128) // NC
+    XL = 2 if NC >= 4 else 1
+    ZC = NC // (2 * XL)
+    PR, LB = N // 2 // ZC, 2 * CW // 128
     RB, WC = T // GROUP, GROUP * CW
     dma = pltpu.SemaphoreType.DMA
     vm = pltpu.VMEM
@@ -577,21 +627,24 @@
         vm((NJ, 2 * HL, SR), F32), vm((NJ, SR, 128), F32), vm((NJ, 2 * HL, SR), F32),
         vm((NJ, N, 2 * CW), F32), vm((NJ, 8, 2 * CW), F32), vm((T, CW), F32),
         vm((SR, HL * SR), BF16), vm((HL * SR, CW), BF16), vm((6 * HL, 2 * CW), BF16),
-        vm((NC, PP, 32, 128), BF16), vm((NC, PP, 32, 128), BF16),
-        vm((NC, PP, 16, 128), BF16), vm((NC, PP, 16, 128), BF16), vm((N, 2 * CW), F32),
+        vm((ZC, LB * PR + 8, 128), F32), vm((ZC, LB * PR + 8, 128), F32),
+        vm((ZC, LB * PR, 128), F32), vm((ZC, LB * PR, 128), F32),
+        vm((LB * PR, 128), F32), vm((LB * PR, 128), F32),
+        vm((N, 2 * CW), F32), vm((N, 2 * CW), F32), vm((8, 2 * CW), F32), vm((8, 2 * CW), F32),
+        vm((N, 2 * CW), F32),
         vm((T, CW), BF16), vm((NJ, RB, CW), BF16), vm((NJ, 8, CW), F32),
         vm((NJ, CW, WC), BF16), vm((RB, WC), F32),
         vm((GROUP, RB, CW), BF16), vm((GROUP, RB, CW), BF16),
-        vm((CW // 128, 16, 128), BF16), vm((NC, PP, 16, 128), F32), vm((RB, CW), F32),
+        vm((RB, CW), F32),
         dma((NJ,)), dma((NJ,)), dma((4,)), dma((2 + NJ,)), dma((NJ,)), dma((NJ,)),
+        dma((NJ,)), dma((NJ,)), dma((4,)), dma((4,)), dma((4,)), dma((4,)),
         dma((NJ,)), dma((NJ,)), dma((NJ,)), dma((NJ,)), dma((NJ,)), dma((NJ,)),
-        dma((NJ,)), dma((NJ,)), dma((NJ,)), dma((NJ,)),
-        dma((NC,)), dma((NC,)), dma((NC,)), dma((NC,)),
+        dma((ZC,)), dma((ZC,)), dma((ZC,)), dma((ZC,)), dma((5,)), dma((5,)),
         dma((NJ,)), dma((NJ,)), dma((GROUP,)), dma((GROUP,)),
         vm(proj_weight.shape, BF16), vm(proj_weight.shape[::-1], BF16), vm((3, H, 128), F32), dma((4,)),
     ]
     return pl.pallas_call(
-        functools.partial(kernel, (NC, NJ, T, CW, D, N, HL, PP)),
+        functools.partial(kernel, (NC, NJ, T, CW, D, N, HL, XL, ZC)),
         out_shape=jax.ShapeDtypeStruct((T, CW), BF16),
         in_specs=[
             pl.BlockSpec(memory_space=pl.ANY if q in (0, 2, 7) else pltpu.VMEM) for q in range(8)

time: 102 us -> 91.5 us (0.90); the launches traced: 101 us -> 91.3 us
  Pallas kernels: 98.8 us -> 89.4 us
    pallas_call x1, Pallas kernels: 98.8 us -> 89.4 us  [shards(): pl.pallas_call(functools.partial(kernel, (NC, NJ, T, CW, D, N, HL, XL, ZC...]
where the time goes in v3:
time: 91.5 us; the launch traced here: 91.3 us
  Pallas kernels  89.4 us (98%)
  local copies, waits for them, and re-layouts  1.87 us (2%)
    pallas_call x1, Pallas kernels, shards(): pl.pallas_call(functools.partial(kernel, (NC, NJ, T, CW, D, N, HL, XL, ZC...  89.4 us
    unnamed x1, local copies, waits for them, and re-layouts  1.87 us

profile of v3, /device:TPU:1, one launch (start us, length us, event | category | flops | bytes accessed | tf_op | source)
XLA Modules:
  0.0 91.3 jit_solution(576481494606808049)
XLA Ops:
  0.0 89.4 %shard_map.82 = bf16[1024,256]{1,0:T(8,128)(2,1)} custom-call(bf16[1024,256]{1,0:T(8,128)(2,1)} %x_ref.1, f32[4,2048]{1,0:T(4,128)} %cw_ref.1, bf16[320,2048]{1,0:T(8,128)(2,1)} %bitcast.5, f32[1,64]{1,0:T(1,128)} %bitcast.7, f32[1,64]{1,0:T(1,128)} %bitcast.8, f32[1,64]{1,0:T(1,128)} %bitcast.9, f32[1,256]{1,0:T(1,128)} %bitcast.6, bf16[256,2048]{1,0:T(8,128)(2,1)} %w_ref.1), custom_call_target="tpu_custom_call" | custom-call | flops 2147483648 | bytes 2097152 | tf_op jit(solution)/shard_map/pallas_call | solution.py:646
  89.4 1.9 %copy.10 = bf16[1024,256]{1,0:T(8,128)(2,1)} copy(bf16[1024,256]{1,0:T(8,128)(2,1)} %shard_map.82) | data formatting | bytes 1048576

commit v4 on v3

--- a/solution.py
+++ b/solution.py
@@ -30,7 +30,7 @@
     dims,
     x_ref, cw_ref, pw_ref, bias_ref, decay_ref, skip_ref, gain_ref, w_ref, out_ref,
     xpad, xe, cbuf, cwr, xf, xr, bb, cc, dtout, dtin, cumr, cumc, ldr, fresh, dch, yacc,
-    mcat, xbd, emat, zs, zr, es, er, xs_, xr_, st_o, ech, dec_me, dec_o, stin, comb_s, comb_r, gall, wbuf, acc, obs, obr, sqs,
+    mcat, xbd, emat, zs, zr, es, er, xs_, xr_, st_o, ech, dec_me, dec_o, stin, comb_s, comb_r, gall, wbuf, acc, obs, obr, sqs, grown, sbs,
     xa_s, xa_r, ha_s, ha_r, g_s, g_r, w_s, w_r, up_s, up_r, dn_s, dn_r, bb_s, bb_r, cc_s, cc_r, dt_s, dt_r,
     zx_s, zx_r, zy_s, zy_r, sb_s, sb_r, cb_s, cb_r, ob_s, ob_r, pwv, pwt, prm, lc,
 ):
@@ -147,10 +147,6 @@
         low = (rest - mid.astype(F32)).astype(BF16)
         return mm(jnp.concatenate([hi, mid, low], axis=0), emat[...], ((0,), (0,)))
 
-    here[2].wait()
-    for b in range(NJ):
-        pwv[b * CW:(b + 1) * CW, :] = pwt[:, b * CW:(b + 1) * CW].T
-
     pl.semaphore_wait(barrier, NJ - 1 + ZC - 1 + XL - 1 + 3 + 2)
 
     def xa(k, jd):
@@ -196,6 +192,10 @@
             vr = vr + rtaps[k:k + 1, :] * cbuf[19 - k:19 - k + SR, :]
         return silu(vf).astype(BF16), silu(vr).astype(BF16)
 
+    here[2].wait()
+    for b in range(NJ):
+        pwv[b * CW:(b + 1) * CW, :] = pwt[:, b * CW:(b + 1) * CW].T
+
     own_cols = pl.ds(pl.multiple_of(j * CW, 128), CW)
 
     def own_conv(c, carry):
@@ -244,24 +244,28 @@
             at(i, dev),
         )
 
+    def halfway(d):
+        return ZC % 2 == 0 and d == ZC // 2 - 1
+
     def up_ring(d, z):
-        part = wbuf.at[:, wrows(z), :]
+        part = wbuf.at[pl.ds(0, NJ // 2 if halfway(d) else NJ), wrows(z), :]
         return rcopy(part, part, up_s.at[d], up_r.at[d], at(zpos(zto(1)), j))
 
     def down_ring(d, z):
-        part = wbuf.at[:, wrows(z), :]
+        first = NJ // 2 if halfway(d) else 0
+        part = wbuf.at[pl.ds(first, NJ - first), wrows(z), :]
         return rcopy(part, part, dn_s.at[d], dn_r.at[d], at(zpos(zfrm(1)), j))
 
     def ring_start(d):
         if d < ZC // 2:
             up_ring(d, zfrm(d)).start()
-        if d < (ZC - 1) // 2:
+        if d < ZC // 2:
             down_ring(d, zto(d)).start()
 
     def ring_wait(d):
         if d < ZC // 2:
             up_ring(d, zfrm(d + 1)).wait_recv()
-        if d < (ZC - 1) // 2:
+        if d < ZC // 2:
             down_ring(d, zto(d + 1)).wait_recv()
 
     def slab(k, carry):
@@ -289,10 +293,19 @@
     pf, pr = lax.fori_loop(
         0, NJ, slab, (jnp.zeros((SR, wide), F32), jnp.zeros((SR, wide), F32))
     )
+    def bbx(k, slot, dev):
+        return rcopy(bb.at[slot], bb.at[slot], bb_s.at[k], bb_r.at[k], at(i, dev))
+
+    def ccx(k, slot, dev):
+        return rcopy(cc.at[slot], cc.at[slot], cc_s.at[k], cc_r.at[k], at(i, dev))
+
+    def dtx(k, slot, dev):
+        return rcopy(dtout.at[dev], dtin.at[slot], dt_s.at[k], dt_r.at[k], at(i, dev))
+
     bb[j, :, 0:N] = pf[:, 0:N].astype(BF16)
     bb[j, :, N:2 * N] = pr[:, 0:N].astype(BF16)
-    cc[j, :, 0:N] = pf[:, N:2 * N].astype(BF16)
-    cc[j, :, N:2 * N] = pr[:, N:2 * N].astype(BF16)
+    for k in range(1, NJ):
+        bbx(k, j, to(k)).start()
     raw = jnp.concatenate([pf[:, 2 * N:], pr[:, 2 * N:]], axis=1).T
     bias = jnp.concatenate([prm[0], prm[0]], axis=0)
     v = raw + bias
@@ -300,39 +313,30 @@
     for q in range(NJ):
         dtout[q, 0:HL, :] = dts[q * HL:(q + 1) * HL, :]
         dtout[q, HL:2 * HL, :] = dts[heads + (NJ - 1 - q) * HL:heads + (NJ - q) * HL, :]
-    dtin[j] = dtout[j]
-
-    def bbx(k, slot, dev):
-        return rcopy(bb.at[slot], bb.at[slot], bb_s.at[k], bb_r.at[k], at(i, dev))
-
-    def ccx(k, slot, dev):
-        return rcopy(cc.at[slot], cc.at[slot], cc_s.at[k], cc_r.at[k], at(i, dev))
-
-    def dtx(k, slot, dev):
-        return rcopy(dtout.at[dev], dtin.at[slot], dt_s.at[k], dt_r.at[k], at(i, dev))
-
     for k in range(1, NJ):
         dtx(k, j, to(k)).start()
-        bbx(k, j, to(k)).start()
+    dtin[j] = dtout[j]
+    cc[j, :, 0:N] = pf[:, N:2 * N].astype(BF16)
+    cc[j, :, N:2 * N] = pr[:, N:2 * N].astype(BF16)
+
+    for h in halo:
+        h.wait_recv()
+
+    @pl.when(i == 0)
+    def _():
+        xpad[0:16, :] = jnp.zeros((16, CW), BF16)
+
+    @pl.when(i == NC - 1)
+    def _():
+        xpad[16 + T:32 + T, :] = jnp.zeros((16, CW), BF16)
+
+    own_conv(0, 0)
+    own_conv(NJ - 1, 0)
 
     for k in range(1, NJ):
         wx(k, frm(k), frm(k)).wait_recv()
     here[3].wait()
     ring_start(0)
-
-    for h in halo:
-        h.wait_recv()
-
-    @pl.when(i == 0)
-    def _():
-        xpad[0:16, :] = jnp.zeros((16, CW), BF16)
-
-    @pl.when(i == NC - 1)
-    def _():
-        xpad[16 + T:32 + T, :] = jnp.zeros((16, CW), BF16)
-
-    own_conv(0, 0)
-    own_conv(NJ - 1, 0)
 
     own = pl.ds(pl.multiple_of(j * HL, 8), HL)
     mirror = pl.ds(pl.multiple_of((NJ - 1 - j) * HL, 8), HL)
@@ -353,6 +357,11 @@
             dtx(k, c, c).wait_recv()
             bbx(k, c, c).wait_recv()
             ccx(k, j, to(k)).start()
+
+        @pl.when(k == NJ // 2)
+        def _():
+            ring_wait(0)
+            ring_start(1)
 
         rows = pl.ds(pl.multiple_of(c * SR, 16), SR)
         dt = dtin[c]
@@ -396,8 +405,6 @@
     ]
     for h in swap:
         h.start()
-    ring_wait(0)
-    ring_start(1)
     for h in swap:
         h.wait_recv()
     mine = pl.ds(pl.multiple_of(core * (N // 2), 8), N // 2)
@@ -455,12 +462,11 @@
             y = y + mm(mcat[...], xbd[...])
             y = y + skips[0:1, d * CW:(d + 1) * CW] * xv.astype(F32)
         yacc[rows, :] = y
+        grown[c] = expand(jnp.exp(cumr[c]))
         return carry
 
     lax.fori_loop(0, 3, inner, 0)
 
-    ring_wait(1)
-    ring_start(2)
     for k in range(1, ZC):
         zx(k, zfrm(k), zfrm(k)).wait_recv()
 
@@ -491,10 +497,10 @@
     for k in range(1, ZC):
         zy(k, zi, zto(k)).start()
     lax.fori_loop(4 if XL > 1 else 3, NJ, inner, 0)
-    ring_wait(2)
-    ring_start(3)
     for k in range(1, ZC):
         zy(k, zfrm(k), zfrm(k)).wait_recv()
+    ring_wait(1)
+    ring_start(2)
     for p in range(ZC):
         for q in range(LB):
             ech[pl.ds(pl.multiple_of(core * (N // 2) + p * PR, 8), PR), q * 128:(q + 1) * 128] = (
@@ -509,29 +515,46 @@
     other_first = fwd_lane == core
     stin[...] = jnp.where(other_first, dec_o[0:1, :] * ech[...] + st_o[...], ech[...])
 
-    def finish(s, carry):
+    def enter(s, carry):
         for d in range(2):
             c = s if d == 0 else NJ - 1 - s
-            rows = pl.ds(pl.multiple_of(c * SR, 16), SR)
             lanes = slice(d * CW, (d + 1) * CW)
             st = stin[:, lanes]
-            z = mm(cc[c, :, d * N:(d + 1) * N], st.astype(BF16))
-            grown = expand(jnp.exp(cumr[c]))[:, lanes]
-            yacc[rows, :] = yacc[rows, :] + grown * z
+            sbs[c, :, lanes] = st.astype(BF16)
             stin[:, lanes] = dch[c, 0:1, lanes] * st + fresh[c, :, lanes]
         return carry
 
-    lax.fori_loop(0, NJ, finish, 0)
-    comb_s[...] = (yacc[...] * gain_ref[...]).astype(BF16)
-
-    def cbx(k, slot, dev):
-        rows = pl.ds(pl.multiple_of(lax.rem(dev, GROUP) * RB, 16), RB)
-        return rcopy(comb_s.at[rows, :], comb_r.at[slot], cb_s.at[k], cb_r.at[k], at(i, dev))
-
-    for k in range(1, NJ):
-        cbx(k, j, to(k)).start()
+    lax.fori_loop(0, NJ, enter, 0)
+
+    HB = RB // 2
+
+    def cbx(h, k, slot, dev):
+        rows = pl.ds(pl.multiple_of(lax.rem(dev, GROUP) * RB + h * HB, 16), HB)
+        return rcopy(
+            comb_s.at[rows, :], comb_r.at[slot, pl.ds(h * HB, HB), :],
+            cb_s.at[h, k], cb_r.at[h, k], at(i, dev),
+        )
+
+    chunks = HB // SR
+    for h in range(2):
+
+        def finish(n, carry):
+            c = (n // chunks) * (2 * chunks) + h * chunks + lax.rem(n, chunks)
+            rows = pl.ds(pl.multiple_of(c * SR, 16), SR)
+            y = yacc[rows, :]
+            for d in range(2):
+                lanes = slice(d * CW, (d + 1) * CW)
+                z = mm(cc[c, :, d * N:(d + 1) * N], sbs[c, :, lanes])
+                y = y + grown[c, :, lanes] * z
+            comb_s[rows, :] = (y * gain_ref[...]).astype(BF16)
+            return carry
+
+        lax.fori_loop(0, NJ // 2, finish, 0)
+        for k in range(1, NJ):
+            cbx(h, k, j, to(k)).start()
     comb_r[j] = comb_s[pl.ds(pl.multiple_of(yy * RB, 16), RB), :]
-
+    ring_wait(2)
+    ring_start(3)
     ring_wait(3)
     half = pl.ds(pl.multiple_of(core * (CW // 2), 16), CW // 2)
     rest = pl.ds(pl.multiple_of((1 - core) * (CW // 2), 16), CW // 2)
@@ -540,41 +563,48 @@
     for k in range(1, NJ):
         s = frm(k)
         rcopy(gall.at[s], gall.at[s], g_s.at[k], g_r.at[k], at(i, s)).wait_recv()
-
-    acc[...] = jnp.zeros((RB, WC), F32)
     rcopy(
         wbuf.at[:, rest, :], wbuf.at[:, rest, :], sb_s.at[4], sb_r.at[4], at(sib, j)
     ).wait_recv()
 
-    def project(k, carry):
-        @pl.when(k > 0)
-        def _():
-            cbx(k, frm(k), frm(k)).wait_recv()
-
-        b = frm(k)
-        acc[...] += mm(comb_r[b], wbuf[b])
-        value = comb_r[b].astype(F32)
-        sqs[...] += value * value * gall[b, 0:1, :]
-        return carry
-
-    sqs[...] = jnp.zeros((RB, CW), F32)
-    lax.fori_loop(0, NJ, project, 0)
-    scale = lax.rsqrt(jnp.sum(sqs[...], axis=1, keepdims=True) / D + EPS)
-    for q in range(GROUP):
-        obs[q] = (acc[:, q * CW:(q + 1) * CW] * scale).astype(BF16)
-
-    def obx(k, slot, dest):
+    def obx(h, k, slot, dest):
+        rows = pl.ds(h * HB, HB)
         return rcopy(
-            obs.at[dest], obr.at[slot], ob_s.at[k], ob_r.at[k], at(i, xh * GROUP + dest)
-        )
-
-    for k in range(1, GROUP):
-        obx(k, yy, lax.rem(yy + k, GROUP)).start()
+            obs.at[dest, rows, :], obr.at[slot, rows, :], ob_s.at[h, k], ob_r.at[h, k],
+            at(i, xh * GROUP + dest),
+        )
+
+    for h in range(2):
+        rows = slice(h * HB, (h + 1) * HB)
+        acc[...] = jnp.zeros((HB, WC), F32)
+        sqs[...] = jnp.zeros((HB, CW), F32)
+
+        def project(k, carry):
+            @pl.when(k > 0)
+            def _():
+                cbx(h, k, frm(k), frm(k)).wait_recv()
+
+            b = frm(k)
+            piece = comb_r[b, rows, :]
+            acc[...] += mm(piece, wbuf[b])
+            value = piece.astype(F32)
+            sqs[...] += value * value * gall[b, 0:1, :]
+            return carry
+
+        lax.fori_loop(0, NJ, project, 0)
+        scale = lax.rsqrt(jnp.sum(sqs[...], axis=1, keepdims=True) / D + EPS)
+        for q in range(GROUP):
+            obs[q, rows, :] = (acc[:, q * CW:(q + 1) * CW] * scale).astype(BF16)
+        for k in range(1, GROUP):
+            obx(h, k, yy, lax.rem(yy + k, GROUP)).start()
     out_ref[pl.ds(pl.multiple_of(yy * RB, 16), RB), :] = obs[yy]
-    for k in range(1, GROUP):
-        s = lax.rem(yy + GROUP - k, GROUP)
-        obx(k, s, s).wait_recv()
-        out_ref[pl.ds(pl.multiple_of(s * RB, 16), RB), :] = obr[s]
+    for h in range(2):
+        for k in range(1, GROUP):
+            s = lax.rem(yy + GROUP - k, GROUP)
+            obx(h, k, s, s).wait_recv()
+            out_ref[pl.ds(pl.multiple_of(s * RB + h * HB, 16), HB), :] = (
+                obr[s, h * HB:(h + 1) * HB, :]
+            )
 
     slab_pre.wait_send()
     slab_post.wait_send()
@@ -588,7 +618,8 @@
         bbx(k, j, to(k)).wait_send()
         ccx(k, j, to(k)).wait_send()
         wx(k, j, to(k)).wait_send()
-        cbx(k, j, to(k)).wait_send()
+        for h in range(2):
+            cbx(h, k, j, to(k)).wait_send()
 
     for k in range(1, ZC):
         zx(k, zi, zto(k)).wait_send()
@@ -599,10 +630,11 @@
     share.wait_send()
     for d in range(ZC // 2):
         up_ring(d, zfrm(d)).wait_send()
-    for d in range((ZC - 1) // 2):
+    for d in range(ZC // 2):
         down_ring(d, zto(d)).wait_send()
-    for k in range(1, GROUP):
-        obx(k, yy, lax.rem(yy + k, GROUP)).wait_send()
+    for h in range(2):
+        for k in range(1, GROUP):
+            obx(h, k, yy, lax.rem(yy + k, GROUP)).wait_send()
 
 
 def shards(x_in, conv_weight, proj_weight, dt_bias, decay_log, skip_gain, norm_gain, out_weight):
@@ -633,14 +665,14 @@
         vm((N, 2 * CW), F32), vm((N, 2 * CW), F32), vm((8, 2 * CW), F32), vm((8, 2 * CW), F32),
         vm((N, 2 * CW), F32),
         vm((T, CW), BF16), vm((NJ, RB, CW), BF16), vm((NJ, 8, CW), F32),
-        vm((NJ, CW, WC), BF16), vm((RB, WC), F32),
+        vm((NJ, CW, WC), BF16), vm((RB // 2, WC), F32),
         vm((GROUP, RB, CW), BF16), vm((GROUP, RB, CW), BF16),
-        vm((RB, CW), F32),
+        vm((RB // 2, CW), F32), vm((NJ, SR, 2 * CW), F32), vm((NJ, N, 2 * CW), BF16),
         dma((NJ,)), dma((NJ,)), dma((4,)), dma((2 + NJ,)), dma((NJ,)), dma((NJ,)),
         dma((NJ,)), dma((NJ,)), dma((4,)), dma((4,)), dma((4,)), dma((4,)),
         dma((NJ,)), dma((NJ,)), dma((NJ,)), dma((NJ,)), dma((NJ,)), dma((NJ,)),
         dma((ZC,)), dma((ZC,)), dma((ZC,)), dma((ZC,)), dma((5,)), dma((5,)),
-        dma((NJ,)), dma((NJ,)), dma((GROUP,)), dma((GROUP,)),
+        dma((2, NJ)), dma((2, NJ)), dma((2, GROUP)), dma((2, GROUP)),
         vm(proj_weight.shape, BF16), vm(proj_weight.shape[::-1], BF16), vm((3, H, 128), F32), dma((4,)),
     ]
     return pl.pallas_call(
@@ -652,7 +684,7 @@
         out_specs=pl.BlockSpec(memory_space=pltpu.VMEM),
         scratch_shapes=scratch,
         compiler_params=pltpu.CompilerParams(
-            collective_id=0, has_side_effects=True, vmem_limit_bytes=62 * 1024 * 1024
+            collective_id=0, has_side_effects=True, vmem_limit_bytes=53 * 1024 * 1024
         ),
         cost_estimate=pl.CostEstimate(
             flops=4 * T * D * CW, bytes_accessed=8 * T * CW, transcendentals=16 * T * SR

time: 91.5 us -> 85 us (0.929)
  Pallas kernels: 89.4 us -> 80.6 us
  local copies, waits for them, and re-layouts: 1.87 us -> 4.2 us
    pallas_call x1, Pallas kernels: 89.4 us -> 80.6 us  [shards(): pl.pallas_call(functools.partial(kernel, (NC, NJ, T, CW, D, N, HL, XL, ZC...]
    unnamed x1 -> x11, local copies, waits for them, and re-layouts: 1.87 us -> 4.2 us
where the time goes in v4:
time: 85 us; the launch traced here: 84.8 us
  Pallas kernels  80.6 us (95%)
  local copies, waits for them, and re-layouts  4.2 us (5%)
    pallas_call x1, Pallas kernels, shards(): pl.pallas_call(functools.partial(kernel, (NC, NJ, T, CW, D, N, HL, XL, ZC...  80.6 us
    unnamed x11, local copies, waits for them, and re-layouts  4.2 us

profile of v4, /device:TPU:1, one launch (start us, length us, event | category | flops | bytes accessed | tf_op | source)
XLA Modules:
  0.0 84.8 jit_solution(2906382582171071882)
XLA Ops:
  0.0 0.0 copy-start
  0.0 0.8 copy-done
  0.8 0.0 copy-start.1
  0.8 0.7 copy-done.1
  1.4 0.0 copy-start.2
  1.4 0.7 copy-done.2
  2.1 0.0 copy-start.3
  2.1 0.7 copy-done.3
  2.8 0.0 copy-start.4
  2.8 0.7 copy-done.4
  3.4 80.6 %shard_map.82 = bf16[1024,256]{1,0:T(8,128)(2,1)S(1)} custom-call(bf16[1024,256]{1,0:T(8,128)(2,1)} %x_ref.1, f32[4,2048]{1,0:T(4,128)S(1)} %copy-done, bf16[320,2048]{1,0:T(8,128)(2,1)} %bitcast.9, f32[1,64]{1,0:T(1,128)S(1)} %bitcast.6, f32[1,64]{1,0:T(1,128)S(1)} %bitcast.7, f32[1,64]{1,0:T(1,128)S(1)} %bitcast.8, f32[1,256]{1,0:T(1,128)S(1)} %bitcast.5, ...), custom_call_target="tpu_custom_call" | custom-call | flops 2147483648 | bytes 2097152 | tf_op jit(solution)/shard_map/pallas_call | solution.py:678
  84.0 0.8 copy.10
Async XLA Ops:
  0.0 0.8 copy-start
  0.8 0.7 copy-start.1
  1.4 0.7 copy-start.2
  2.1 0.7 copy-start.3
  2.8 0.7 copy-start.4

commit v5 on v4

--- a/solution.py
+++ b/solution.py
@@ -28,11 +28,12 @@
 
 def kernel(
     dims,
-    x_ref, cw_ref, pw_ref, bias_ref, decay_ref, skip_ref, gain_ref, w_ref, out_ref,
-    xpad, xe, cbuf, cwr, xf, xr, bb, cc, dtout, dtin, cumr, cumc, ldr, fresh, dch, yacc,
+    x_ref, cw_hbm, pw_ref, bias_hbm, decay_hbm, skip_hbm, gain_hbm, w_ref, out_ref,
+    xpad, xe, cbuf, cwr, xf, xr, bb, cc, dtout, dtin, cumr, fresh, dch, yacc,
     mcat, xbd, emat, zs, zr, es, er, xs_, xr_, st_o, ech, dec_me, dec_o, stin, comb_s, comb_r, gall, wbuf, acc, obs, obr, sqs, grown, sbs,
     xa_s, xa_r, ha_s, ha_r, g_s, g_r, w_s, w_r, up_s, up_r, dn_s, dn_r, bb_s, bb_r, cc_s, cc_r, dt_s, dt_r,
-    zx_s, zx_r, zy_s, zy_r, sb_s, sb_r, cb_s, cb_r, ob_s, ob_r, pwv, pwt, prm, lc,
+    zx_s, zx_r, zy_s, zy_r, sb_s, sb_r, cb_s, cb_r, ob_s, ob_r, pwv, pwr, pwt, prm, lc,
+    cw_ref, bias_ref, decay_ref, skip_ref, gain_ref, oc,
 ):
     NC, NJ, T, CW, D, N, HL, XL, ZC = dims
     SR = T // NJ
@@ -56,50 +57,20 @@
         return {"ctx": ci, "chan": cj}
 
     def to(k):
-        return lax.rem(j + k, NJ)
+        return lax.rem(xh + k // GROUP, 2) * GROUP + lax.rem(yy + lax.rem(k, GROUP), GROUP)
 
     def frm(k):
-        return lax.rem(j + NJ - k, NJ)
+        return (
+            lax.rem(xh + k // GROUP, 2) * GROUP
+            + lax.rem(yy + GROUP - lax.rem(k, GROUP), GROUP)
+        )
+
+    far_first = (6, 5, 7, 4, 2, 1, 3)
 
     def rcopy(src, dst, ss, rs, dev):
         return pltpu.make_async_remote_copy(
             src_ref=src, dst_ref=dst, send_sem=ss, recv_sem=rs, device_id=dev, device_id_type=MESH
         )
-
-    barrier = pltpu.get_barrier_semaphore()
-
-    def hail(dev):
-        pl.semaphore_signal(barrier, inc=1, device_id=dev, device_id_type=MESH)
-
-    for k in range(1, NJ):
-        hail(at(i, to(k)))
-
-    def zpos(z):
-        return xlo * (2 * ZC) + z * 2 + core
-
-    def zto(k):
-        return lax.rem(zi + k, ZC)
-
-    def zfrm(k):
-        return lax.rem(zi + ZC - k, ZC)
-
-    for k in range(1, ZC):
-        hail(at(zpos(zto(k)), j))
-    across = lax.rem(i + 2 * ZC, NC)
-    if XL > 1:
-        hail(at(across, j))
-    for c in (sib, prev_i, next_i):
-        hail(at(c, j))
-
-    @pl.when(j == 0)
-    def _():
-        for q in range(NJ):
-            hail(at(prev_i, q))
-
-    @pl.when(j == NJ - 1)
-    def _():
-        for q in range(NJ):
-            hail(at(next_i, q))
 
     def win(jd):
         return pl.multiple_of(jnp.clip(SR * jd - 16, 0, T - SR - 32), 16)
@@ -118,8 +89,53 @@
             w_ref.at[wrows(zi), own_wide], wbuf.at[j, wrows(zi), :], lc.at[3]
         ),
     ]
-    for h in here:
+    small = [
+        pltpu.make_async_copy(src, dst, lc.at[4 + q])
+        for q, (src, dst) in enumerate((
+            (cw_hbm, cw_ref), (bias_hbm, bias_ref), (decay_hbm, decay_ref),
+            (skip_hbm, skip_ref), (gain_hbm, gain_ref),
+        ))
+    ]
+    for h in small + here:
         h.start()
+
+    barrier = pltpu.get_barrier_semaphore()
+
+    def hail(dev):
+        pl.semaphore_signal(barrier, inc=1, device_id=dev, device_id_type=MESH)
+
+    for k in range(1, NJ):
+        hail(at(i, to(k)))
+
+    def zpos(z):
+        return xlo * (2 * ZC) + z * 2 + core
+
+    def zto(k):
+        return lax.rem(zi + k, ZC)
+
+    def zfrm(k):
+        return lax.rem(zi + ZC - k, ZC)
+
+    for k in range(1, ZC):
+        hail(at(zpos(zto(k)), j))
+    across = lax.rem(i + 2 * ZC, NC)
+    if XL > 1:
+        hail(at(across, j))
+    for c in (sib, prev_i, next_i):
+        hail(at(c, j))
+
+    @pl.when(j == 0)
+    def _():
+        for q in range(NJ):
+            hail(at(prev_i, q))
+
+    @pl.when(j == NJ - 1)
+    def _():
+        for q in range(NJ):
+            hail(at(next_i, q))
+
+    for h in small:
+        h.wait()
     gall[j] = jnp.broadcast_to(1.0 / (gain_ref[...] * gain_ref[...]), (8, CW))
     heads = HL * NJ
     eye = iota((heads, heads), 0) == iota((heads, heads), 1)
@@ -140,12 +156,15 @@
     target = jnp.where(head_of < HL, head_of, 3 * HL - 1 - head_of)
     emat[...] = jnp.where(head_row == target, 1.0, 0.0).astype(BF16)
 
-    def expand(rows):
+    def terms(rows):
         hi = rows.astype(BF16)
         rest = rows - hi.astype(F32)
         mid = rest.astype(BF16)
         low = (rest - mid.astype(F32)).astype(BF16)
-        return mm(jnp.concatenate([hi, mid, low], axis=0), emat[...], ((0,), (0,)))
+        return jnp.concatenate([hi, mid, low], axis=0)
+
+    def expand(rows):
+        return mm(terms(rows), emat[...], ((0,), (0,)))
 
     pl.semaphore_wait(barrier, NJ - 1 + ZC - 1 + XL - 1 + 3 + 2)
 
@@ -174,7 +193,7 @@
     )
     slab_pre.start()
     slab_post.start()
-    for k in range(1, NJ):
+    for k in far_first:
         xa(k, to(k)).start()
     for h in halo:
         h.start()
@@ -194,7 +213,9 @@
 
     here[2].wait()
     for b in range(NJ):
-        pwv[b * CW:(b + 1) * CW, :] = pwt[:, b * CW:(b + 1) * CW].T
+        block = pwt[:, b * CW:(b + 1) * CW].T
+        pwv[b * CW:(b + 1) * CW, :] = block
+        pwr[(NJ - 1 - b) * CW:(NJ - b) * CW, :] = mm(anti_b, block).astype(BF16)
 
     own_cols = pl.ds(pl.multiple_of(j * CW, 128), CW)
 
@@ -273,7 +294,7 @@
 
         @pl.when(k == NJ // 2)
         def _():
-            for q in range(1, NJ):
+            for q in far_first:
                 wx(q, j, to(q)).start()
 
         @pl.when(k > 0)
@@ -284,9 +305,8 @@
         cols = pl.ds(pl.multiple_of(b * CW, 128), CW)
         cbuf[...] = xe[b, pl.ds(start, SR + 32), :].astype(F32)
         f, r = conv_pair(cw_ref[:, cols], cwr[:, cols])
-        flipped = mm(r, anti_b).astype(BF16)
-        pf = pf + mm(f, pwv[pl.ds(pl.multiple_of(b * CW, 128), CW), :])
-        pr = pr + mm(flipped, pwv[pl.ds(pl.multiple_of((NJ - 1 - b) * CW, 128), CW), :])
+        pf = pf + mm(f, pwv[cols, :])
+        pr = pr + mm(r, pwr[cols, :])
         return pf, pr
 
     wide = pwv.shape[1]
@@ -304,7 +324,7 @@
 
     bb[j, :, 0:N] = pf[:, 0:N].astype(BF16)
     bb[j, :, N:2 * N] = pr[:, 0:N].astype(BF16)
-    for k in range(1, NJ):
+    for k in far_first:
         bbx(k, j, to(k)).start()
     raw = jnp.concatenate([pf[:, 2 * N:], pr[:, 2 * N:]], axis=1).T
     bias = jnp.concatenate([prm[0], prm[0]], axis=0)
@@ -313,7 +333,7 @@
     for q in range(NJ):
         dtout[q, 0:HL, :] = dts[q * HL:(q + 1) * HL, :]
         dtout[q, HL:2 * HL, :] = dts[heads + (NJ - 1 - q) * HL:heads + (NJ - q) * HL, :]
-    for k in range(1, NJ):
+    for k in far_first:
         dtx(k, j, to(k)).start()
     dtin[j] = dtout[j]
     cc[j, :, 0:N] = pf[:, N:2 * N].astype(BF16)
@@ -345,47 +365,51 @@
         return jnp.concatenate([prm[which, own, :], prm[which, mirror, :]], axis=0)
 
     rate = -jnp.exp(own_rows(1))
-    up = jnp.where(iota((SR, SR), 0) <= iota((SR, SR), 1), 1.0, 0.0).astype(F32)
-    down = jnp.where(iota((SR, SR), 0) >= iota((SR, SR), 1), 1.0, 0.0).astype(F32)
+    src, dst = iota((SR, 2 * SR), 0), iota((SR, 2 * SR), 1)
+    sums = jnp.where(dst < SR, dst - src, src - dst + SR) >= 0
+    sums = jnp.where(sums, 1.0, 0.0).astype(BF16)
     is_fwd = iota((2 * HL, SR), 0) < HL
-
-    def states(k, total):
+    chunk_lane = iota((2 * HL, SR), 1)
+
+    def states(k, ends):
         c = frm(k)
 
         @pl.when(k > 0)
         def _():
             dtx(k, c, c).wait_recv()
             bbx(k, c, c).wait_recv()
-            ccx(k, j, to(k)).start()
 
         @pl.when(k == NJ // 2)
         def _():
             ring_wait(0)
             ring_start(1)
 
+        @pl.when(k == NJ - 1)
+        def _():
+            for q in far_first:
+                ccx(q, j, to(q)).start()
+
         rows = pl.ds(pl.multiple_of(c * SR, 16), SR)
         dt = dtin[c]
         a = dt * rate
-        cum = jnp.where(
-            is_fwd,
-            mm(a, up, precision=lax.Precision.HIGHEST),
-            mm(a, down, precision=lax.Precision.HIGHEST),
-        )
-        end = jnp.broadcast_to(jnp.sum(a, axis=1, keepdims=True), (2 * HL, SR))
+        run = mm(terms(a), sums)
+        run = run[0:2 * HL] + run[2 * HL:4 * HL] + run[4 * HL:6 * HL]
+        cum = jnp.where(is_fwd, run[:, 0:SR], run[:, SR:2 * SR])
+        end = jnp.sum(a, axis=1, keepdims=True)
         cumr[c] = cum
-        ldr[c] = cum - jnp.log(dt)
-        cumc[c] = jnp.concatenate([cum, jnp.zeros((SR - 2 * HL, SR), F32)], axis=0).T
         tail = expand(jnp.exp(end - cum) * dt)
-        whole = expand(jnp.exp(end))
-        dch[c] = whole[0:8, :]
         tf = (xf[rows, :].astype(F32) * tail[:, 0:CW]).astype(BF16)
         tr = (xr[rows, :].astype(F32) * tail[:, CW:2 * CW]).astype(BF16)
         fresh[c, :, 0:CW] = mm(bb[c, :, 0:N], tf, ((0,), (0,)))
         fresh[c, :, CW:2 * CW] = mm(bb[c, :, N:2 * N], tr, ((0,), (0,)))
-        return total + end
-
-    total = lax.fori_loop(0, NJ, states, jnp.zeros((2 * HL, SR), F32))
-    dec_me[...] = expand(jnp.exp(total))[0:8, :]
+        return jnp.where(chunk_lane == c, end, ends)
+
+    ends = lax.fori_loop(0, NJ, states, jnp.zeros((2 * HL, SR), F32))
+    ends = jnp.where(chunk_lane == NJ, jnp.sum(ends, axis=1, keepdims=True), ends)
+    whole = expand(jnp.exp(ends))
+    for c in range(NJ):
+        dch[c] = jnp.broadcast_to(whole[c:c + 1, :], (8, 2 * CW))
+    dec_me[...] = jnp.broadcast_to(whole[NJ:NJ + 1, :], (8, 2 * CW))
 
     stin[...] = jnp.zeros((N, 2 * CW), F32)
 
@@ -446,8 +470,9 @@
             ccx(k, c, c).wait_recv()
 
         rows = pl.ds(pl.multiple_of(c * SR, 16), SR)
-        cols = cumc[c]
-        lds = ldr[c]
+        cum = cumr[c]
+        cols = jnp.concatenate([cum, jnp.zeros((SR - 2 * HL, SR), F32)], axis=0).T
+        lds = cum - jnp.log(dtin[c])
         y = jnp.zeros((SR, CW), F32)
         for d, (xs, mask) in enumerate(((xf, low), (xr, upp))):
             xv = xs[rows, :]
@@ -462,7 +487,7 @@
             y = y + mm(mcat[...], xbd[...])
             y = y + skips[0:1, d * CW:(d + 1) * CW] * xv.astype(F32)
         yacc[rows, :] = y
-        grown[c] = expand(jnp.exp(cumr[c]))
+        grown[c] = expand(jnp.exp(cum))
         return carry
 
     lax.fori_loop(0, 3, inner, 0)
@@ -550,7 +575,7 @@
             return carry
 
         lax.fori_loop(0, NJ // 2, finish, 0)
-        for k in range(1, NJ):
+        for k in far_first:
             cbx(h, k, j, to(k)).start()
     comb_r[j] = comb_s[pl.ds(pl.multiple_of(yy * RB, 16), RB), :]
     ring_wait(2)
@@ -597,14 +622,22 @@
             obs[q, rows, :] = (acc[:, q * CW:(q + 1) * CW] * scale).astype(BF16)
         for k in range(1, GROUP):
             obx(h, k, yy, lax.rem(yy + k, GROUP)).start()
-    out_ref[pl.ds(pl.multiple_of(yy * RB, 16), RB), :] = obs[yy]
+    def place_out(n, src, s, h, size):
+        rows = pl.ds(pl.multiple_of(s * RB + h * HB, 16), size)
+        return pltpu.make_async_copy(src, out_ref.at[rows, :], oc.at[n])
+
+    outs = [place_out(0, obs.at[yy], yy, 0, RB)]
+    outs[0].start()
     for h in range(2):
         for k in range(1, GROUP):
             s = lax.rem(yy + GROUP - k, GROUP)
             obx(h, k, s, s).wait_recv()
-            out_ref[pl.ds(pl.multiple_of(s * RB + h * HB, 16), HB), :] = (
-                obr[s, h * HB:(h + 1) * HB, :]
+            outs.append(
+                place_out(h * GROUP + k, obr.at[s, pl.ds(h * HB, HB), :], s, h, HB)
             )
+            outs[-1].start()
+    for h in outs:
+        h.wait()
 
     slab_pre.wait_send()
     slab_post.wait_send()
@@ -656,7 +689,7 @@
         vm((4, D), F32), vm((T, CW), BF16), vm((T, CW), BF16),
         vm((NJ, SR, 2 * N), BF16), vm((NJ, SR, 2 * N), BF16),
         vm((NJ, 2 * HL, SR), F32), vm((NJ, 2 * HL, SR), F32),
-        vm((NJ, 2 * HL, SR), F32), vm((NJ, SR, 128), F32), vm((NJ, 2 * HL, SR), F32),
+        vm((NJ, 2 * HL, SR), F32),
         vm((NJ, N, 2 * CW), F32), vm((NJ, 8, 2 * CW), F32), vm((T, CW), F32),
         vm((SR, HL * SR), BF16), vm((HL * SR, CW), BF16), vm((6 * HL, 2 * CW), BF16),
         vm((ZC, LB * PR + 8, 128), F32), vm((ZC, LB * PR + 8, 128), F32),
@@ -673,18 +706,18 @@
         dma((NJ,)), dma((NJ,)), dma((NJ,)), dma((NJ,)), dma((NJ,)), dma((NJ,)),
         dma((ZC,)), dma((ZC,)), dma((ZC,)), dma((ZC,)), dma((5,)), dma((5,)),
         dma((2, NJ)), dma((2, NJ)), dma((2, GROUP)), dma((2, GROUP)),
-        vm(proj_weight.shape, BF16), vm(proj_weight.shape[::-1], BF16), vm((3, H, 128), F32), dma((4,)),
+        vm(proj_weight.shape, BF16), vm(proj_weight.shape, BF16),
+        vm(proj_weight.shape[::-1], BF16), vm((3, H, 128), F32), dma((9,)),
+        vm((4, D), F32), vm((1, H), F32), vm((1, H), F32), vm((1, H), F32), vm((1, CW), F32), dma((2 * GROUP,)),
     ]
     return pl.pallas_call(
         functools.partial(kernel, (NC, NJ, T, CW, D, N, HL, XL, ZC)),
         out_shape=jax.ShapeDtypeStruct((T, CW), BF16),
-        in_specs=[
-            pl.BlockSpec(memory_space=pl.ANY if q in (0, 2, 7) else pltpu.VMEM) for q in range(8)
-        ],
-        out_specs=pl.BlockSpec(memory_space=pltpu.VMEM),
+        in_specs=[pl.BlockSpec(memory_space=pl.ANY)] * 8,
+        out_specs=pl.BlockSpec(memory_space=pl.ANY),
         scratch_shapes=scratch,
         compiler_params=pltpu.CompilerParams(
-            collective_id=0, has_side_effects=True, vmem_limit_bytes=53 * 1024 * 1024
+            collective_id=0, has_side_effects=True, vmem_limit_bytes=62 * 1024 * 1024
         ),
         cost_estimate=pl.CostEstimate(
             flops=4 * T * D * CW, bytes_accessed=8 * T * CW, transcendentals=16 * T * SR

time: 85 us -> 84.3 us (level)
  local copies, waits for them, and re-layouts: 4.2 us -> 1.87 us
  Pallas kernels: 80.6 us -> 82 us
    unnamed x11 -> x1, local copies, waits for them, and re-layouts: 4.2 us -> 1.87 us
    pallas_call x1, Pallas kernels: 80.6 us -> 82 us  [shards(): pl.pallas_call(functools.partial(kernel, (NC, NJ, T, CW, D, N, HL, XL, ZC...]
where the time goes in v5:
time: 84.3 us; the launch traced here: 83.8 us
  Pallas kernels  82 us (97%)
  local copies, waits for them, and re-layouts  1.87 us (2%)
    pallas_call x1, Pallas kernels, shards(): pl.pallas_call(functools.partial(kernel, (NC, NJ, T, CW, D, N, HL, XL, ZC...  82 us
    unnamed x1, local copies, waits for them, and re-layouts  1.87 us

profile of v5, /device:TPU:1, one launch (start us, length us, event | category | flops | bytes accessed | tf_op | source)
XLA Modules:
  0.0 83.8 jit_solution(4514671189551286304)
XLA Ops:
  0.0 82.0 %shard_map.82 = bf16[1024,256]{1,0:T(8,128)(2,1)} custom-call(bf16[1024,256]{1,0:T(8,128)(2,1)} %x_ref.1, f32[4,2048]{1,0:T(4,128)} %cw_hbm.1, bf16[320,2048]{1,0:T(8,128)(2,1)} %bitcast.5, f32[1,64]{1,0:T(1,128)} %bitcast.7, f32[1,64]{1,0:T(1,128)} %bitcast.8, f32[1,64]{1,0:T(1,128)} %bitcast.9, f32[1,256]{1,0:T(1,128)} %bitcast.6, bf16[256,2048]{1,0:T(8,128)(2,1)} %w_ref.1), custom_call_target="tpu_custom_call" | custom-call | flops 2147483648 | bytes 2097152 | tf_op jit(solution)/shard_map/pallas_call | solution.py:713
  82.0 1.9 %copy.10 = bf16[1024,256]{1,0:T(8,128)(2,1)} copy(bf16[1024,256]{1,0:T(8,128)(2,1)} %shard_map.82) | data formatting | bytes 1048576

commit v6 on v5

--- a/solution.py
+++ b/solution.py
@@ -384,9 +384,14 @@
             ring_wait(0)
             ring_start(1)
 
+        @pl.when(k == 1)
+        def _():
+            for q in range(1, GROUP):
+                ccx(q, j, to(q)).start()
+
         @pl.when(k == NJ - 1)
         def _():
-            for q in far_first:
+            for q in range(GROUP, NJ):
                 ccx(q, j, to(q)).start()
 
         rows = pl.ds(pl.multiple_of(c * SR, 16), SR)
@@ -438,14 +443,19 @@
     other_last = fwd_lane == 1 - core
     pair = jnp.where(other_last, d_o * s_me + s_o, d_me * s_o + s_me)
     d_pair = jnp.broadcast_to(d_me * d_o, (8, 2 * CW))
-    place = iota((8, 128), 0)
-    d_tile = jnp.zeros((8, 128), F32)
+    place = iota((16, 128), 0)
+    d_tile = jnp.zeros((16, 128), F32)
     for q in range(LB):
-        d_tile = jnp.where(place == q, d_pair[:, q * 128:(q + 1) * 128], d_tile)
+        d = d_pair[:, q * 128:(q + 1) * 128][0:1, :]
+        hi = d.astype(BF16).astype(F32)
+        mid = (d - hi).astype(BF16).astype(F32)
+        for t, term in enumerate((hi, mid, d - hi - mid)):
+            d_tile = jnp.where(place == t * LB + q, term, d_tile)
+    d_tile = d_tile.astype(BF16)
     for p in range(ZC):
-        for q in range(LB):
-            zs[p, q * PR:(q + 1) * PR, :] = pair[p * PR:(p + 1) * PR, q * 128:(q + 1) * 128]
-        zs[p, LB * PR:LB * PR + 8, :] = d_tile
+        blocks = [pair[p * PR:(p + 1) * PR, q * 128:(q + 1) * 128] for q in range(LB)]
+        zs[p, 0:LB * PR, :] = jnp.concatenate(blocks, axis=0).astype(BF16)
+        zs[p, LB * PR:LB * PR + 16, :] = d_tile
     zr[zi] = zs[zi]
 
     def zx(k, slot, z):
@@ -495,29 +505,41 @@
     for k in range(1, ZC):
         zx(k, zfrm(k), zfrm(k)).wait_recv()
 
-    def chain(q, e, keep):
+    pieces, decays = [], []
+    for z in range(ZC):
+        whole = zr[z].astype(F32)
+        pieces.append(whole[0:LB * PR])
+        tile = whole[LB * PR:LB * PR + 16]
+        decays.append([
+            tile[q:q + 1] + tile[LB + q:LB + q + 1] + tile[2 * LB + q:2 * LB + q + 1]
+            for q in range(LB)
+        ])
+
+    def chain(q, e):
         order = range(ZC) if q < LB // 2 else range(ZC - 1, -1, -1)
-        rows = slice(q * PR, (q + 1) * PR)
+        before = [None] * ZC
         for z in order:
-            if keep:
-                es[z, rows, :] = e
-            e = zr[z, LB * PR + q:LB * PR + q + 1, :] * e + zr[z, rows, :]
-        return e
+            before[z] = e
+            e = decays[z][q] * e + pieces[z][q * PR:(q + 1) * PR]
+        return before, e
 
     zero = jnp.zeros((PR, 128), F32)
     if XL > 1:
         for q in range(LB):
-            xs_[q * PR:(q + 1) * PR, :] = chain(q, zero, False)
+            xs_[q * PR:(q + 1) * PR, :] = chain(q, zero)[1]
         cross = rcopy(xs_, xr_, sb_s.at[2], sb_r.at[2], at(across, j))
         cross.start()
         lax.fori_loop(3, 4, inner, 0)
         cross.wait_recv()
+    before = []
     for q in range(LB):
         start_from = zero
         if XL > 1:
             takes = xlo == 1 if q < LB // 2 else xlo == 0
             start_from = jnp.where(takes, xr_[q * PR:(q + 1) * PR, :], 0.0)
-        chain(q, start_from, True)
+        before.append(chain(q, start_from)[0])
+    for z in range(ZC):
+        es[z] = jnp.concatenate([before[q][z] for q in range(LB)], axis=0).astype(BF16)
     er[zi] = es[zi]
     for k in range(1, ZC):
         zy(k, zi, zto(k)).start()
@@ -527,9 +549,10 @@
     ring_wait(1)
     ring_start(2)
     for p in range(ZC):
+        piece = er[p].astype(F32)
         for q in range(LB):
             ech[pl.ds(pl.multiple_of(core * (N // 2) + p * PR, 8), PR), q * 128:(q + 1) * 128] = (
-                er[p, q * PR:(q + 1) * PR, :]
+                piece[q * PR:(q + 1) * PR, :]
             )
     halves = rcopy(ech.at[mine, :], ech.at[mine, :], sb_s.at[3], sb_r.at[3], at(sib, j))
     halves.start()
@@ -692,8 +715,8 @@
         vm((NJ, 2 * HL, SR), F32),
         vm((NJ, N, 2 * CW), F32), vm((NJ, 8, 2 * CW), F32), vm((T, CW), F32),
         vm((SR, HL * SR), BF16), vm((HL * SR, CW), BF16), vm((6 * HL, 2 * CW), BF16),
-        vm((ZC, LB * PR + 8, 128), F32), vm((ZC, LB * PR + 8, 128), F32),
-        vm((ZC, LB * PR, 128), F32), vm((ZC, LB * PR, 128), F32),
+        vm((ZC, LB * PR + 16, 128), BF16), vm((ZC, LB * PR + 16, 128), BF16),
+        vm((ZC, LB * PR, 128), BF16), vm((ZC, LB * PR, 128), BF16),
         vm((LB * PR, 128), F32), vm((LB * PR, 128), F32),
         vm((N, 2 * CW), F32), vm((N, 2 * CW), F32), vm((8, 2 * CW), F32), vm((8, 2 * CW), F32),
         vm((N, 2 * CW), F32),

time: 84.3 us -> 82 us (0.973)
  Pallas kernels: 82 us -> 79.9 us
    pallas_call x1, Pallas kernels: 82 us -> 79.9 us  [shards(): pl.pallas_call(functools.partial(kernel, (NC, NJ, T, CW, D, N, HL, XL, ZC...]
where the time goes in v6:
time: 82 us; the launch traced here: 81.8 us
  Pallas kernels  79.9 us (97%)
  local copies, waits for them, and re-layouts  1.87 us (2%)
    pallas_call x1, Pallas kernels, shards(): pl.pallas_call(functools.partial(kernel, (NC, NJ, T, CW, D, N, HL, XL, ZC...  79.9 us
    unnamed x1, local copies, waits for them, and re-layouts  1.87 us

profile of v6, /device:TPU:1, one launch (start us, length us, event | category | flops | bytes accessed | tf_op | source)
XLA Modules:
  0.0 81.8 jit_solution(6192341109935300025)
XLA Ops:
  0.0 79.9 %shard_map.82 = bf16[1024,256]{1,0:T(8,128)(2,1)} custom-call(bf16[1024,256]{1,0:T(8,128)(2,1)} %x_ref.1, f32[4,2048]{1,0:T(4,128)} %cw_hbm.1, bf16[320,2048]{1,0:T(8,128)(2,1)} %bitcast.5, f32[1,64]{1,0:T(1,128)} %bitcast.7, f32[1,64]{1,0:T(1,128)} %bitcast.8, f32[1,64]{1,0:T(1,128)} %bitcast.9, f32[1,256]{1,0:T(1,128)} %bitcast.6, bf16[256,2048]{1,0:T(8,128)(2,1)} %w_ref.1), custom_call_target="tpu_custom_call" | custom-call | flops 2147483648 | bytes 2097152 | tf_op jit(solution)/shard_map/pallas_call | solution.py:736
  80.0 1.9 %copy.10 = bf16[1024,256]{1,0:T(8,128)(2,1)} copy(bf16[1024,256]{1,0:T(8,128)(2,1)} %shard_map.82) | data formatting | bytes 1048576

commit v7 on v6

--- a/solution.py
+++ b/solution.py
@@ -316,6 +316,9 @@
     def bbx(k, slot, dev):
         return rcopy(bb.at[slot], bb.at[slot], bb_s.at[k], bb_r.at[k], at(i, dev))
 
+    def relay(k, slot, dev):
+        return rcopy(bb.at[slot], bb.at[slot], bb_s.at[GROUP + k], bb_r.at[GROUP + k], at(i, dev))
+
     def ccx(k, slot, dev):
         return rcopy(cc.at[slot], cc.at[slot], cc_s.at[k], cc_r.at[k], at(i, dev))
 
@@ -324,7 +327,7 @@
 
     bb[j, :, 0:N] = pf[:, 0:N].astype(BF16)
     bb[j, :, N:2 * N] = pr[:, 0:N].astype(BF16)
-    for k in far_first:
+    for k in (GROUP, 2, 1, 3):
         bbx(k, j, to(k)).start()
     raw = jnp.concatenate([pf[:, 2 * N:], pr[:, 2 * N:]], axis=1).T
     bias = jnp.concatenate([prm[0], prm[0]], axis=0)
@@ -353,6 +356,10 @@
     own_conv(0, 0)
     own_conv(NJ - 1, 0)
 
+    bbx(GROUP, frm(GROUP), frm(GROUP)).wait_recv()
+    for k in (2, 1, 3):
+        relay(k, to(GROUP), to(k)).start()
+
     for k in range(1, NJ):
         wx(k, frm(k), frm(k)).wait_recv()
     here[3].wait()
@@ -377,7 +384,14 @@
         @pl.when(k > 0)
         def _():
             dtx(k, c, c).wait_recv()
+
+        @pl.when(jnp.logical_and(k > 0, k < GROUP))
+        def _():
             bbx(k, c, c).wait_recv()
+
+        @pl.when(k > GROUP)
+        def _():
+            relay(k - GROUP, c, c).wait_recv()
 
         @pl.when(k == NJ // 2)
         def _():
@@ -504,6 +518,8 @@
 
     for k in range(1, ZC):
         zx(k, zfrm(k), zfrm(k)).wait_recv()
+    ring_wait(1)
+    ring_start(2)
 
     pieces, decays = [], []
     for z in range(ZC):
@@ -546,8 +562,8 @@
     lax.fori_loop(4 if XL > 1 else 3, NJ, inner, 0)
     for k in range(1, ZC):
         zy(k, zfrm(k), zfrm(k)).wait_recv()
-    ring_wait(1)
-    ring_start(2)
+    ring_wait(2)
+    ring_start(3)
     for p in range(ZC):
         piece = er[p].astype(F32)
         for q in range(LB):
@@ -601,8 +617,6 @@
         for k in far_first:
             cbx(h, k, j, to(k)).start()
     comb_r[j] = comb_s[pl.ds(pl.multiple_of(yy * RB, 16), RB), :]
-    ring_wait(2)
-    ring_start(3)
     ring_wait(3)
     half = pl.ds(pl.multiple_of(core * (CW // 2), 16), CW // 2)
     rest = pl.ds(pl.multiple_of((1 - core) * (CW // 2), 16), CW // 2)
@@ -671,7 +685,10 @@
     for k in range(1, NJ):
         xa(k, to(k)).wait_send()
         dtx(k, j, to(k)).wait_send()
-        bbx(k, j, to(k)).wait_send()
+        if k <= GROUP:
+            bbx(k, j, to(k)).wait_send()
+        else:
+            relay(k - GROUP, to(GROUP), to(k - GROUP)).wait_send()
         ccx(k, j, to(k)).wait_send()
         wx(k, j, to(k)).wait_send()
         for h in range(2):

time: 82 us -> 82.4 us (level)
  no operation moved by 1% of the time
where the time goes in v7:
time: 82.4 us; the launch traced here: 82.2 us
  Pallas kernels  80.3 us (97%)
  local copies, waits for them, and re-layouts  1.87 us (2%)
    pallas_call x1, Pallas kernels, shards(): pl.pallas_call(functools.partial(kernel, (NC, NJ, T, CW, D, N, HL, XL, ZC...  80.3 us
    unnamed x1, local copies, waits for them, and re-layouts  1.87 us

profile of v7, /device:TPU:1, one launch (start us, length us, event | category | flops | bytes accessed | tf_op | source)
XLA Modules:
  0.0 82.2 jit_solution(2960008709599540714)
XLA Ops:
  0.0 80.3 %shard_map.82 = bf16[1024,256]{1,0:T(8,128)(2,1)} custom-call(bf16[1024,256]{1,0:T(8,128)(2,1)} %x_ref.1, f32[4,2048]{1,0:T(4,128)} %cw_hbm.1, bf16[320,2048]{1,0:T(8,128)(2,1)} %bitcast.5, f32[1,64]{1,0:T(1,128)} %bitcast.7, f32[1,64]{1,0:T(1,128)} %bitcast.8, f32[1,64]{1,0:T(1,128)} %bitcast.9, f32[1,256]{1,0:T(1,128)} %bitcast.6, bf16[256,2048]{1,0:T(8,128)(2,1)} %w_ref.1), custom_call_target="tpu_custom_call" | custom-call | flops 2147483648 | bytes 2097152 | tf_op jit(solution)/shard_map/pallas_call | solution.py:753
  80.4 1.9 %copy.10 = bf16[1024,256]{1,0:T(8,128)(2,1)} copy(bf16[1024,256]{1,0:T(8,128)(2,1)} %shard_map.82) | data formatting | bytes 1048576

commit v8 on v7

--- a/solution.py
+++ b/solution.py
@@ -195,6 +195,43 @@
     slab_post.start()
     for k in far_first:
         xa(k, to(k)).start()
+    def wx(k, slot, dev):
+        cols = pl.ds(pl.multiple_of((dev // GROUP) * WC, 128), WC)
+        return rcopy(
+            w_ref.at[wrows(zi), cols], wbuf.at[slot, wrows(zi), :], w_s.at[k], w_r.at[k],
+            at(i, dev),
+        )
+
+    def wrelay(k, slot, dev):
+        part = wbuf.at[slot, wrows(zi), :]
+        return rcopy(part, part, w_s.at[GROUP + k], w_r.at[GROUP + k], at(i, dev))
+
+    def halfway(d):
+        return ZC % 2 == 0 and d == ZC // 2 - 1
+
+    def up_ring(d, z):
+        part = wbuf.at[pl.ds(0, NJ // 2 if halfway(d) else NJ), wrows(z), :]
+        return rcopy(part, part, up_s.at[d], up_r.at[d], at(zpos(zto(1)), j))
+
+    def down_ring(d, z):
+        first = NJ // 2 if halfway(d) else 0
+        part = wbuf.at[pl.ds(first, NJ - first), wrows(z), :]
+        return rcopy(part, part, dn_s.at[d], dn_r.at[d], at(zpos(zfrm(1)), j))
+
+    def ring_start(d):
+        if d < ZC // 2:
+            up_ring(d, zfrm(d)).start()
+        if d < ZC // 2:
+            down_ring(d, zto(d)).start()
+
+    def ring_wait(d):
+        if d < ZC // 2:
+            up_ring(d, zfrm(d + 1)).wait_recv()
+        if d < ZC // 2:
+            down_ring(d, zto(d + 1)).wait_recv()
+
+    for k in (GROUP, 2, 1, 3):
+        wx(k, j, to(k)).start()
     for h in halo:
         h.start()
     gains = [
@@ -258,44 +295,14 @@
     start = pl.multiple_of(SR * j - win(j), 16)
     here[1].wait()
 
-    def wx(k, slot, dev):
-        cols = pl.ds(pl.multiple_of((dev // GROUP) * WC, 128), WC)
-        return rcopy(
-            w_ref.at[wrows(zi), cols], wbuf.at[slot, wrows(zi), :], w_s.at[k], w_r.at[k],
-            at(i, dev),
-        )
-
-    def halfway(d):
-        return ZC % 2 == 0 and d == ZC // 2 - 1
-
-    def up_ring(d, z):
-        part = wbuf.at[pl.ds(0, NJ // 2 if halfway(d) else NJ), wrows(z), :]
-        return rcopy(part, part, up_s.at[d], up_r.at[d], at(zpos(zto(1)), j))
-
-    def down_ring(d, z):
-        first = NJ // 2 if halfway(d) else 0
-        part = wbuf.at[pl.ds(first, NJ - first), wrows(z), :]
-        return rcopy(part, part, dn_s.at[d], dn_r.at[d], at(zpos(zfrm(1)), j))
-
-    def ring_start(d):
-        if d < ZC // 2:
-            up_ring(d, zfrm(d)).start()
-        if d < ZC // 2:
-            down_ring(d, zto(d)).start()
-
-    def ring_wait(d):
-        if d < ZC // 2:
-            up_ring(d, zfrm(d + 1)).wait_recv()
-        if d < ZC // 2:
-            down_ring(d, zto(d + 1)).wait_recv()
-
     def slab(k, carry):
         pf, pr = carry
 
-        @pl.when(k == NJ // 2)
-        def _():
-            for q in far_first:
-                wx(q, j, to(q)).start()
+        @pl.when(k == GROUP)
+        def _():
+            wx(GROUP, frm(GROUP), frm(GROUP)).wait_recv()
+            for q in (2, 1, 3):
+                wrelay(q, to(GROUP), to(q)).start()
 
         @pl.when(k > 0)
         def _():
@@ -356,14 +363,15 @@
     own_conv(0, 0)
     own_conv(NJ - 1, 0)
 
+    for k in range(1, GROUP):
+        wx(k, frm(k), frm(k)).wait_recv()
+        wrelay(k, frm(GROUP + k), frm(k)).wait_recv()
+    here[3].wait()
+    ring_start(0)
+
     bbx(GROUP, frm(GROUP), frm(GROUP)).wait_recv()
     for k in (2, 1, 3):
         relay(k, to(GROUP), to(k)).start()
-
-    for k in range(1, NJ):
-        wx(k, frm(k), frm(k)).wait_recv()
-    here[3].wait()
-    ring_start(0)
 
     own = pl.ds(pl.multiple_of(j * HL, 8), HL)
     mirror = pl.ds(pl.multiple_of((NJ - 1 - j) * HL, 8), HL)
@@ -393,7 +401,7 @@
         def _():
             relay(k - GROUP, c, c).wait_recv()
 
-        @pl.when(k == NJ // 2)
+        @pl.when(k == GROUP + 2)
         def _():
             ring_wait(0)
             ring_start(1)
@@ -403,7 +411,7 @@
             for q in range(1, GROUP):
                 ccx(q, j, to(q)).start()
 
-        @pl.when(k == NJ - 1)
+        @pl.when(k == GROUP + 1)
         def _():
             for q in range(GROUP, NJ):
                 ccx(q, j, to(q)).start()
@@ -518,8 +526,6 @@
 
     for k in range(1, ZC):
         zx(k, zfrm(k), zfrm(k)).wait_recv()
-    ring_wait(1)
-    ring_start(2)
 
     pieces, decays = [], []
     for z in range(ZC):
@@ -562,8 +568,8 @@
     lax.fori_loop(4 if XL > 1 else 3, NJ, inner, 0)
     for k in range(1, ZC):
         zy(k, zfrm(k), zfrm(k)).wait_recv()
-    ring_wait(2)
-    ring_start(3)
+    ring_wait(1)
+    ring_start(2)
     for p in range(ZC):
         piece = er[p].astype(F32)
         for q in range(LB):
@@ -617,6 +623,8 @@
         for k in far_first:
             cbx(h, k, j, to(k)).start()
     comb_r[j] = comb_s[pl.ds(pl.multiple_of(yy * RB, 16), RB), :]
+    ring_wait(2)
+    ring_start(3)
     ring_wait(3)
     half = pl.ds(pl.multiple_of(core * (CW // 2), 16), CW // 2)
     rest = pl.ds(pl.multiple_of((1 - core) * (CW // 2), 16), CW // 2)
@@ -690,7 +698,10 @@
         else:
             relay(k - GROUP, to(GROUP), to(k - GROUP)).wait_send()
         ccx(k, j, to(k)).wait_send()
-        wx(k, j, to(k)).wait_send()
+        if k <= GROUP:
+            wx(k, j, to(k)).wait_send()
+        else:
+            wrelay(k - GROUP, to(GROUP), to(k - GROUP)).wait_send()
         for h in range(2):
             cbx(h, k, j, to(k)).wait_send()
 

time: 82.4 us -> 78.9 us (0.958)
  Pallas kernels: 80.3 us -> 76.9 us
    pallas_call x1, Pallas kernels: 80.3 us -> 76.9 us  [shards(): pl.pallas_call(functools.partial(kernel, (NC, NJ, T, CW, D, N, HL, XL, ZC...]
where the time goes in v8:
time: 78.9 us; the launch traced here: 78.8 us
  Pallas kernels  76.9 us (97%)
  local copies, waits for them, and re-layouts  1.87 us (2%)
    pallas_call x1, Pallas kernels, shards(): pl.pallas_call(functools.partial(kernel, (NC, NJ, T, CW, D, N, HL, XL, ZC...  76.9 us
    unnamed x1, local copies, waits for them, and re-layouts  1.87 us

profile of v8, /device:TPU:1, one launch (start us, length us, event | category | flops | bytes accessed | tf_op | source)
XLA Modules:
  0.0 78.8 jit_solution(8638633242386840958)
XLA Ops:
  0.0 76.9 %shard_map.82 = bf16[1024,256]{1,0:T(8,128)(2,1)} custom-call(bf16[1024,256]{1,0:T(8,128)(2,1)} %x_ref.1, f32[4,2048]{1,0:T(4,128)} %cw_hbm.1, bf16[320,2048]{1,0:T(8,128)(2,1)} %bitcast.5, f32[1,64]{1,0:T(1,128)} %bitcast.7, f32[1,64]{1,0:T(1,128)} %bitcast.8, f32[1,64]{1,0:T(1,128)} %bitcast.9, f32[1,256]{1,0:T(1,128)} %bitcast.6, bf16[256,2048]{1,0:T(8,128)(2,1)} %w_ref.1), custom_call_target="tpu_custom_call" | custom-call | flops 2147483648 | bytes 2097152 | tf_op jit(solution)/shard_map/pallas_call | solution.py:764
  76.9 1.9 %copy.10 = bf16[1024,256]{1,0:T(8,128)(2,1)} copy(bf16[1024,256]{1,0:T(8,128)(2,1)} %shard_map.82) | data formatting | bytes 1048576

commit v9 on v8

--- a/solution.py
+++ b/solution.py
@@ -240,12 +240,12 @@
     for g in gains:
         g.start()
 
-    def conv_pair(taps, rtaps):
-        vf = taps[0:1, :] * cbuf[13:13 + SR, :]
-        vr = rtaps[0:1, :] * cbuf[19:19 + SR, :]
+    def conv_pair(taps, rtaps, slot=0):
+        vf = taps[0:1, :] * cbuf[slot, 13:13 + SR, :]
+        vr = rtaps[0:1, :] * cbuf[slot, 19:19 + SR, :]
         for k in range(1, 4):
-            vf = vf + taps[k:k + 1, :] * cbuf[13 + k:13 + k + SR, :]
-            vr = vr + rtaps[k:k + 1, :] * cbuf[19 - k:19 - k + SR, :]
+            vf = vf + taps[k:k + 1, :] * cbuf[slot, 13 + k:13 + k + SR, :]
+            vr = vr + rtaps[k:k + 1, :] * cbuf[slot, 19 - k:19 - k + SR, :]
         return silu(vf).astype(BF16), silu(vr).astype(BF16)
 
     here[2].wait()
@@ -258,7 +258,7 @@
 
     def own_conv(c, carry):
         rows = pl.ds(pl.multiple_of(c * SR, 16), SR)
-        cbuf[...] = xpad[pl.ds(pl.multiple_of(c * SR, 16), SR + 32), :].astype(F32)
+        cbuf[0] = xpad[pl.ds(pl.multiple_of(c * SR, 16), SR + 32), :].astype(F32)
         f, r = conv_pair(cw_ref[:, own_cols], cwr[:, own_cols])
         xf[rows, :] = f
         xr[rows, :] = r
@@ -295,31 +295,34 @@
     start = pl.multiple_of(SR * j - win(j), 16)
     here[1].wait()
 
+    def block_proj(k, slot, carry):
+        pf, pr = carry
+        b = frm(k)
+        cols = pl.ds(pl.multiple_of(b * CW, 128), CW)
+        cbuf[slot] = xe[b, pl.ds(start, SR + 32), :].astype(F32)
+        f, r = conv_pair(cw_ref[:, cols], cwr[:, cols], slot)
+        pf = pf + mm(f, pwv[cols, :])
+        pr = pr + mm(r, pwr[cols, :])
+        return pf, pr
+
     def slab(k, carry):
-        pf, pr = carry
-
-        @pl.when(k == GROUP)
-        def _():
-            wx(GROUP, frm(GROUP), frm(GROUP)).wait_recv()
-            for q in (2, 1, 3):
-                wrelay(q, to(GROUP), to(q)).start()
-
         @pl.when(k > 0)
         def _():
             xa_in(k).wait_recv()
 
-        b = frm(k)
-        cols = pl.ds(pl.multiple_of(b * CW, 128), CW)
-        cbuf[...] = xe[b, pl.ds(start, SR + 32), :].astype(F32)
-        f, r = conv_pair(cw_ref[:, cols], cwr[:, cols])
-        pf = pf + mm(f, pwv[cols, :])
-        pr = pr + mm(r, pwr[cols, :])
-        return pf, pr
+        return block_proj(k, 0, carry)
 
     wide = pwv.shape[1]
     pf, pr = lax.fori_loop(
-        0, NJ, slab, (jnp.zeros((SR, wide), F32), jnp.zeros((SR, wide), F32))
+        0, GROUP, slab, (jnp.zeros((SR, wide), F32), jnp.zeros((SR, wide), F32))
     )
+    wx(GROUP, frm(GROUP), frm(GROUP)).wait_recv()
+    for q in (2, 1, 3):
+        wrelay(q, to(GROUP), to(q)).start()
+    for k in range(GROUP, NJ):
+        xa_in(k).wait_recv()
+    for k in range(GROUP, NJ):
+        pf, pr = block_proj(k, k % 2, (pf, pr))
     def bbx(k, slot, dev):
         return rcopy(bb.at[slot], bb.at[slot], bb_s.at[k], bb_r.at[k], at(i, dev))
 
@@ -590,7 +593,9 @@
             c = s if d == 0 else NJ - 1 - s
             lanes = slice(d * CW, (d + 1) * CW)
             st = stin[:, lanes]
-            sbs[c, :, lanes] = st.astype(BF16)
+            top = st.astype(BF16)
+            sbs[c, 0:N, lanes] = top
+            sbs[c, N:2 * N, lanes] = (st - top.astype(F32)).astype(BF16)
             stin[:, lanes] = dch[c, 0:1, lanes] * st + fresh[c, :, lanes]
         return carry
 
@@ -614,7 +619,8 @@
             y = yacc[rows, :]
             for d in range(2):
                 lanes = slice(d * CW, (d + 1) * CW)
-                z = mm(cc[c, :, d * N:(d + 1) * N], sbs[c, :, lanes])
+                cv = cc[c, :, d * N:(d + 1) * N]
+                z = mm(jnp.concatenate([cv, cv], axis=1), sbs[c, :, lanes])
                 y = y + grown[c, :, lanes] * z
             comb_s[rows, :] = (y * gain_ref[...]).astype(BF16)
             return carry
@@ -736,7 +742,7 @@
     dma = pltpu.SemaphoreType.DMA
     vm = pltpu.VMEM
     scratch = [
-        vm((T + 32, CW), BF16), vm((NJ, SR + 64, CW), BF16), vm((SR + 32, CW), F32),
+        vm((T + 32, CW), BF16), vm((NJ, SR + 64, CW), BF16), vm((2, SR + 32, CW), F32),
         vm((4, D), F32), vm((T, CW), BF16), vm((T, CW), BF16),
         vm((NJ, SR, 2 * N), BF16), vm((NJ, SR, 2 * N), BF16),
         vm((NJ, 2 * HL, SR), F32), vm((NJ, 2 * HL, SR), F32),
@@ -751,7 +757,7 @@
         vm((T, CW), BF16), vm((NJ, RB, CW), BF16), vm((NJ, 8, CW), F32),
         vm((NJ, CW, WC), BF16), vm((RB // 2, WC), F32),
         vm((GROUP, RB, CW), BF16), vm((GROUP, RB, CW), BF16),
-        vm((RB // 2, CW), F32), vm((NJ, SR, 2 * CW), F32), vm((NJ, N, 2 * CW), BF16),
+        vm((RB // 2, CW), F32), vm((NJ, SR, 2 * CW), F32), vm((NJ, 2 * N, 2 * CW), BF16),
         dma((NJ,)), dma((NJ,)), dma((4,)), dma((2 + NJ,)), dma((NJ,)), dma((NJ,)),
         dma((NJ,)), dma((NJ,)), dma((4,)), dma((4,)), dma((4,)), dma((4,)),
         dma((NJ,)), dma((NJ,)), dma((NJ,)), dma((NJ,)), dma((NJ,)), dma((NJ,)),

time: 78.9 us -> 77.6 us (0.984)
  Pallas kernels: 76.9 us -> 75.6 us
    pallas_call x1, Pallas kernels: 76.9 us -> 75.6 us  [shards(): pl.pallas_call(functools.partial(kernel, (NC, NJ, T, CW, D, N, HL, XL, ZC...]
where the time goes in v9:
time: 77.6 us; the launch traced here: 77.5 us
  Pallas kernels  75.6 us (97%)
  local copies, waits for them, and re-layouts  1.87 us (2%)
    pallas_call x1, Pallas kernels, shards(): pl.pallas_call(functools.partial(kernel, (NC, NJ, T, CW, D, N, HL, XL, ZC...  75.6 us
    unnamed x1, local copies, waits for them, and re-layouts  1.87 us

profile of v9, /device:TPU:1, one launch (start us, length us, event | category | flops | bytes accessed | tf_op | source)
XLA Modules:
  0.0 77.5 jit_solution(16422817286114953090)
XLA Ops:
  0.0 75.6 %shard_map.82 = bf16[1024,256]{1,0:T(8,128)(2,1)} custom-call(bf16[1024,256]{1,0:T(8,128)(2,1)} %x_ref.1, f32[4,2048]{1,0:T(4,128)} %cw_hbm.1, bf16[320,2048]{1,0:T(8,128)(2,1)} %bitcast.5, f32[1,64]{1,0:T(1,128)} %bitcast.7, f32[1,64]{1,0:T(1,128)} %bitcast.8, f32[1,64]{1,0:T(1,128)} %bitcast.9, f32[1,256]{1,0:T(1,128)} %bitcast.6, bf16[256,2048]{1,0:T(8,128)(2,1)} %w_ref.1), custom_call_target="tpu_custom_call" | custom-call | flops 2147483648 | bytes 2097152 | tf_op jit(solution)/shard_map/pallas_call | solution.py:770
  75.6 1.9 %copy.10 = bf16[1024,256]{1,0:T(8,128)(2,1)} copy(bf16[1024,256]{1,0:T(8,128)(2,1)} %shard_map.82) | data formatting | bytes 1048576

commit v10 on v9

--- a/solution.py
+++ b/solution.py
@@ -389,36 +389,7 @@
     is_fwd = iota((2 * HL, SR), 0) < HL
     chunk_lane = iota((2 * HL, SR), 1)
 
-    def states(k, ends):
-        c = frm(k)
-
-        @pl.when(k > 0)
-        def _():
-            dtx(k, c, c).wait_recv()
-
-        @pl.when(jnp.logical_and(k > 0, k < GROUP))
-        def _():
-            bbx(k, c, c).wait_recv()
-
-        @pl.when(k > GROUP)
-        def _():
-            relay(k - GROUP, c, c).wait_recv()
-
-        @pl.when(k == GROUP + 2)
-        def _():
-            ring_wait(0)
-            ring_start(1)
-
-        @pl.when(k == 1)
-        def _():
-            for q in range(1, GROUP):
-                ccx(q, j, to(q)).start()
-
-        @pl.when(k == GROUP + 1)
-        def _():
-            for q in range(GROUP, NJ):
-                ccx(q, j, to(q)).start()
-
+    def chunk_state(c, ends):
         rows = pl.ds(pl.multiple_of(c * SR, 16), SR)
         dt = dtin[c]
         a = dt * rate
@@ -434,7 +405,33 @@
         fresh[c, :, CW:2 * CW] = mm(bb[c, :, N:2 * N], tr, ((0,), (0,)))
         return jnp.where(chunk_lane == c, end, ends)
 
-    ends = lax.fori_loop(0, NJ, states, jnp.zeros((2 * HL, SR), F32))
+    def states(k, ends):
+        c = frm(k)
+
+        @pl.when(k > 0)
+        def _():
+            dtx(k, c, c).wait_recv()
+            bbx(k, c, c).wait_recv()
+
+        @pl.when(k == 1)
+        def _():
+            for q in range(1, GROUP):
+                ccx(q, j, to(q)).start()
+
+        return chunk_state(c, ends)
+
+    ends = lax.fori_loop(0, GROUP, states, jnp.zeros((2 * HL, SR), F32))
+    for k in range(GROUP, NJ):
+        dtx(k, frm(k), frm(k)).wait_recv()
+        if k > GROUP:
+            relay(k - GROUP, frm(k), frm(k)).wait_recv()
+    for k in range(GROUP, NJ):
+        ccx(k, j, to(k)).start()
+    for k in range(GROUP, NJ):
+        if k == GROUP + 2:
+            ring_wait(0)
+            ring_start(1)
+        ends = chunk_state(frm(k), ends)
     ends = jnp.where(chunk_lane == NJ, jnp.sum(ends, axis=1, keepdims=True), ends)
     whole = expand(jnp.exp(ends))
     for c in range(NJ):
@@ -655,19 +652,28 @@
         acc[...] = jnp.zeros((HB, WC), F32)
         sqs[...] = jnp.zeros((HB, CW), F32)
 
+        def multiply(b):
+            piece = comb_r[b, rows, :]
+            value = piece.astype(F32)
+            return mm(piece, wbuf[b]), value * value * gall[b, 0:1, :]
+
         def project(k, carry):
             @pl.when(k > 0)
             def _():
                 cbx(h, k, frm(k), frm(k)).wait_recv()
 
-            b = frm(k)
-            piece = comb_r[b, rows, :]
-            acc[...] += mm(piece, wbuf[b])
-            value = piece.astype(F32)
-            sqs[...] += value * value * gall[b, 0:1, :]
+            product, square = multiply(frm(k))
+            acc[...] += product
+            sqs[...] += square
             return carry
 
-        lax.fori_loop(0, NJ, project, 0)
+        lax.fori_loop(0, GROUP, project, 0)
+        for k in range(GROUP, NJ):
+            cbx(h, k, frm(k), frm(k)).wait_recv()
+        for k in range(GROUP, NJ):
+            product, square = multiply(frm(k))
+            acc[...] += product
+            sqs[...] += square
         scale = lax.rsqrt(jnp.sum(sqs[...], axis=1, keepdims=True) / D + EPS)
         for q in range(GROUP):
             obs[q, rows, :] = (acc[:, q * CW:(q + 1) * CW] * scale).astype(BF16)

time: 77.6 us -> 78.1 us (level)
  no operation moved by 1% of the time
where the time goes in v10:
time: 78.1 us; the launch traced here: 78 us
  Pallas kernels  76.1 us (97%)
  local copies, waits for them, and re-layouts  1.87 us (2%)
    pallas_call x1, Pallas kernels, shards(): pl.pallas_call(functools.partial(kernel, (NC, NJ, T, CW, D, N, HL, XL, ZC...  76.1 us
    unnamed x1, local copies, waits for them, and re-layouts  1.87 us

profile of v10, /device:TPU:1, one launch (start us, length us, event | category | flops | bytes accessed | tf_op | source)
XLA Modules:
  0.0 78.0 jit_solution(13905157552312652959)
XLA Ops:
  0.0 76.1 %shard_map.82 = bf16[1024,256]{1,0:T(8,128)(2,1)} custom-call(bf16[1024,256]{1,0:T(8,128)(2,1)} %x_ref.1, f32[4,2048]{1,0:T(4,128)} %cw_hbm.1, bf16[320,2048]{1,0:T(8,128)(2,1)} %bitcast.5, f32[1,64]{1,0:T(1,128)} %bitcast.7, f32[1,64]{1,0:T(1,128)} %bitcast.8, f32[1,64]{1,0:T(1,128)} %bitcast.9, f32[1,256]{1,0:T(1,128)} %bitcast.6, bf16[256,2048]{1,0:T(8,128)(2,1)} %w_ref.1), custom_call_target="tpu_custom_call" | custom-call | flops 2147483648 | bytes 2097152 | tf_op jit(solution)/shard_map/pallas_call | solution.py:776
  76.1 1.9 %copy.10 = bf16[1024,256]{1,0:T(8,128)(2,1)} copy(bf16[1024,256]{1,0:T(8,128)(2,1)} %shard_map.82) | data formatting | bytes 1048576
